TPU v7x, 256 devices: a whole 4x4x8 slice. The times are simulated.
256 devices in a mesh: group: 4 (over z_lo), tensor: 64 (over x, y, z_hi, core).
Axes of the slice: x: 4, y: 4, z: 8 (z_hi: 2, z_lo: 4; z = z_hi * 4 + z_lo), core: 2. Of those that a mesh axis runs over, the one named last changes fastest.
Arguments:
- query_init: bfloat16 [5120, 8192], P(('group', 'tensor'))
- query_first: bfloat16 [5120, 8192], P(('group', 'tensor')), as said below
- query_second: bfloat16 [5120, 8192], P(('group', 'tensor'))
- key_init: bfloat16 [5120, 1024], P(('group', 'tensor'))
- key_first: bfloat16 [5120, 1024], P(('group', 'tensor'))
- key_second: bfloat16 [5120, 1024], P(('group', 'tensor'))
- value_init: bfloat16 [5120, 1024], P(('group', 'tensor'))
- value_first: bfloat16 [5120, 1024], P(('group', 'tensor'))
- value_second: bfloat16 [5120, 1024], P(('group', 'tensor'))
- output_init: bfloat16 [8192, 5120], P(('group', 'tensor'))
- output_first: bfloat16 [8192, 5120], P(('group', 'tensor'))
- output_second: bfloat16 [8192, 5120], P(('group', 'tensor'))
- hidden_rows: bfloat16 [16, 5120], P('group'), may hold values from -6 to 6
- cache_keys: bfloat16 [16, 8, 4096, 128], P('group', None, 'tensor'), may hold values from -256 to 256, as said below
- cache_values: bfloat16 [16, 8, 4096, 128], P('group', None, 'tensor'), may hold values from -6 to 6
- positions: int32 [16], P('group'), may hold values from 4096 to 8191
- lengths: int32 [16], P('group'), may hold values from 1 to 4096, as said below
Outputs:
- attended: bfloat16 [16, 5120], P('group')
Inputs may be any that keep to these rules, and one draw needn't show every extreme that they name: `query_first`: each of the three arrays of a projection has the same shape; the policies differ from the initialization by task vectors of full rank. `cache_keys`: cached keys are real-valued and bounded. `lengths`: some row has exactly 4096 filled slots.
All inputs are finite; a program needn't handle non-finite values.
Results may differ from a plain program's by a relative error of at most 0.012.
The roundings to bfloat16 on the way count: a program that leaves them out, or rounds other values in their place, can miss the bound.
Values may be sent and summed in bfloat16 or wider, within the bound.
A program may use at most 64 MiB of HBM per device.

v0:
```python
import math

import jax
import jax.numpy as jnp
from jax import lax
from jax.sharding import PartitionSpec as P

blend = 0.5
rope_base = 1000000.0


def combined_all(value, axis, join):
    pieces = jax.tree.map(lambda part: lax.all_gather(part, axis), value)
    head = jax.tree.map(lambda part: part[0], pieces)
    tail = jax.tree.map(lambda part: part[1:], pieces)
    so_far, _ = lax.scan(lambda so_far, share: (join(so_far, share), None), head, tail)
    return so_far


def rotate(values, positions):
    half = values.shape[-1] // 2
    steps = jnp.arange(half, dtype=jnp.float32) * (2.0 / values.shape[-1])
    freq = rope_base ** (-steps)
    angle = positions.astype(jnp.float32)[:, None] * freq[None, :]
    cosine = jnp.cos(angle)[:, None, :]
    sine = jnp.sin(angle)[:, None, :]
    first = values[..., :half]
    second = values[..., half:]
    return jnp.concatenate(
        [first * cosine - second * sine, second * cosine + first * sine], axis=-1
    )


def task_terms(init, first, second):
    base = init.astype(jnp.float32)
    delta_a = first.astype(jnp.float32) - base
    delta_b = second.astype(jnp.float32) - base
    local = jnp.stack(
        [jnp.sum(delta_a * delta_a), jnp.sum(delta_b * delta_b), jnp.sum(delta_a * delta_b)]
    )
    return (base, delta_a, delta_b, local)


def combine_task(base, delta_a, delta_b, sums):
    cosine = sums[2] / jnp.sqrt(sums[0] * sums[1] + 1e-06)
    angle = jnp.arccos(cosine)
    inverse = 1.0 / jnp.sin(angle)
    merged = (
        base
        + jnp.sin((1.0 - blend) * angle) * inverse * delta_a
        + jnp.sin(blend * angle) * inverse * delta_b
    )
    return merged.astype(jnp.bfloat16)


def merge_parts(left, right):
    top = jnp.maximum(left[0], right[0])
    left_factor = jnp.exp(left[0] - top)
    right_factor = jnp.exp(right[0] - top)
    return (
        top,
        left[1] * left_factor + right[1] * right_factor,
        left[2] * left_factor[..., None] + right[2] * right_factor[..., None],
    )


def shards(
    query_init,
    query_first,
    query_second,
    key_init,
    key_first,
    key_second,
    value_init,
    value_first,
    value_second,
    output_init,
    output_first,
    output_second,
    hidden_rows,
    cache_keys,
    cache_values,
    positions,
    lengths,
):
    pieces = [
        task_terms(query_init, query_first, query_second),
        task_terms(key_init, key_first, key_second),
        task_terms(value_init, value_first, value_second),
        task_terms(output_init, output_first, output_second),
    ]
    merged = []
    for piece in pieces:
        sums = lax.psum(piece[3], ("group", "tensor"))
        merged.append(combine_task(piece[0], piece[1], piece[2], sums))
    groups = lax.axis_size("group")
    parts = lax.axis_size("tensor")
    mine = lax.axis_index("tensor")

    def own_columns(matrix):
        count, width = matrix.shape
        block = width // (groups * parts)
        shaped = matrix.reshape(count, groups, parts, block)
        taken = lax.dynamic_slice_in_dim(shaped, mine, 1, 2)
        return taken.reshape(count, groups * block)

    rows_here = hidden_rows.shape[0]
    kv_heads = cache_keys.shape[1]
    span = cache_keys.shape[2]
    head_dim = cache_keys.shape[3]
    query_width = query_init.shape[1]
    heads_all = query_width // head_dim
    out_rows = merged[3]
    inputs_own = own_columns(hidden_rows)
    query_rows, key_rows, value_rows, out_rows = (
        lax.all_gather(merged[0], "group", axis=0, tiled=True),
        lax.all_gather(merged[1], "group", axis=0, tiled=True),
        lax.all_gather(merged[2], "group", axis=0, tiled=True),
        lax.all_gather(merged[3], "group", axis=0, tiled=True),
    )
    query_part = jnp.dot(inputs_own, query_rows, preferred_element_type=jnp.float32)
    key_part = jnp.dot(inputs_own, key_rows, preferred_element_type=jnp.float32)
    value_part = jnp.dot(inputs_own, value_rows, preferred_element_type=jnp.float32)
    query_full, key_full, value_full = lax.psum((query_part, key_part, value_part), "tensor")
    query = (
        rotate(query_full.reshape(rows_here, heads_all, head_dim), positions)
        .astype(jnp.bfloat16)
        .reshape(rows_here, query_width)
    )
    new_key = rotate(key_full.reshape(rows_here, kv_heads, head_dim), positions).astype(
        jnp.bfloat16
    )
    new_value = value_full.astype(jnp.bfloat16).reshape(rows_here, kv_heads, head_dim)
    grouped = query.reshape(rows_here, kv_heads, heads_all // kv_heads, head_dim)
    scale = 1.0 / math.sqrt(head_dim)
    scores = (
        jnp.einsum("rkgd,rkpd->rkgp", grouped, cache_keys, preferred_element_type=jnp.float32)
        * scale
    )
    slots = mine * span + jnp.arange(span, dtype=jnp.int32)
    valid = (slots[None, :] < lengths[:, None])[:, None, None, :]
    peak = jnp.max(jnp.where(valid, scores, -1e30), axis=-1)
    weights = jnp.where(valid, jnp.exp(scores - peak[..., None]), 0.0).astype(jnp.bfloat16)
    total = jnp.sum(weights.astype(jnp.float32), axis=-1)
    mixed = jnp.einsum("rkgp,rkpd->rkgd", weights, cache_values, preferred_element_type=jnp.float32)
    peak, total, mixed = combined_all((peak, total, mixed), "tensor", merge_parts)
    own = jnp.einsum("rkgd,rkd->rkg", grouped, new_key, preferred_element_type=jnp.float32) * scale
    top = jnp.maximum(peak, own)
    old_factor = jnp.exp(peak - top)
    own_factor = jnp.exp(own - top)
    denom = total * old_factor + own_factor
    heads = (
        mixed * old_factor[..., None]
        + own_factor[..., None] * new_value.astype(jnp.float32)[:, :, None, :]
    ) / denom[..., None]
    heads = heads.astype(jnp.bfloat16).reshape(rows_here, query_width)
    out_part = jnp.dot(own_columns(heads), out_rows, preferred_element_type=jnp.float32)
    return lax.psum(out_part, "tensor").astype(jnp.bfloat16)


def solution(mesh):
    in_specs = (
        P(("group", "tensor"), None),
        P(("group", "tensor"), None),
        P(("group", "tensor"), None),
        P(("group", "tensor"), None),
        P(("group", "tensor"), None),
        P(("group", "tensor"), None),
        P(("group", "tensor"), None),
        P(("group", "tensor"), None),
        P(("group", "tensor"), None),
        P(("group", "tensor"), None),
        P(("group", "tensor"), None),
        P(("group", "tensor"), None),
        P("group", None),
        P("group", None, "tensor", None),
        P("group", None, "tensor", None),
        P("group"),
        P("group"),
    )
    out_specs = P("group", None)
    return jax.shard_map(shards, mesh=mesh, in_specs=in_specs, out_specs=out_specs, check_vma=False)
```

profile of v0, /device:TPU:1, one launch (start us, length us, event | category | flops | bytes accessed | tf_op | source)
XLA Modules:
  0.0 2018.0 jit_solution(15099167437257542574)
XLA Ops:
  6.6 2.4 multiply_reduce_fusion.2
  9.0 2.0 pad_maximum_fusion.3
  10.9 1.6 multiply_reduce_fusion.11
  12.5 2.0 pad_maximum_fusion.4
  14.5 1.6 multiply_reduce_fusion.8
  16.1 2.0 pad_maximum_fusion.5
  18.0 2.0 multiply_reduce_fusion.5
  20.1 2.0 pad_maximum_fusion.6
  22.0 81.4 %all-reduce = (f32[3]{0:T(128)S(1)}, f32[3]{0:T(128)S(1)}, f32[3]{0:T(128)S(1)}, f32[3]{0:T(128)S(1)}) all-reduce(f32[3]{0:T(128)S(1)} %pad_maximum_fusion.3, f32[3]{0:T(128)S(1)} %pad_maximum_fusion.4, f32[3]{0:T(128)S(1)} %pad_maximum_fusion.5, f32[3]{0:T(128)S(1)} %pad_maximum_fusion.6), channel_id=1, replica_groups=mesh['group'=4,'tensor'=64] {'group','tensor'}, use_global_device_ids=true, to_apply=%region_3.0 | all-reduce | flops 12 | bytes 96 | tf_op jit(solution)/shard_map/psum | solution.py:94
  108.3 35.9 %all-gather.14.cloned.1.call-done = bf16[4,20,8192]{2,1,0:T(8,128)(2,1)} async-done(((bf16[1,20,8192]{2,1,0:T(8,128)(2,1)}), bf16[4,20,8192]{2,1,0:T(8,128)(2,1)}) %all-gather.14.cloned.1.call-update) | async-done | bytes 1310736 | tf_op jit(solution)/shard_map/all_gather | solution.py:116
  144.2 1.5 reshape.150
  146.9 715.3 %all-reduce.4.cloned.1.call-done = f32[4,64,128]{2,1,0:T(8,128)} async-done(((f32[4,64,128]{2,1,0:T(8,128)}), f32[4,64,128]{2,1,0:T(8,128)}) %all-reduce.4.cloned.1.call-update) | async-done | bytes 131088 | tf_op jit(solution)/shard_map/psum | solution.py:124
  862.2 1.1 fusion.12
  873.4 11.1 all-gather.4
  884.5 12.1 all-gather.5
  897.0 402.9 %all-reduce.1 = (f32[4,8,128]{2,1,0:T(8,128)S(1)}, bf16[4,1024]{1,0:T(4,128)(2,1)S(1)}) all-reduce(f32[4,8,128]{2,1,0:T(8,128)S(1)} %bitcast.84, f32[4,1024]{1,0:T(4,128)S(1)} %fusion.31), channel_id=1, replica_groups=mesh['group'=4,'tensor'=64] {'tensor'}, use_global_device_ids=true, to_apply=%region_13.0 | all-reduce | flops 8192 | bytes 57344 | tf_op jit(solution)/shard_map/psum | solution.py:124
  1300.3 122.0 %all-gather = f32[256,8,8]{2,1,0:T(8,128)S(1)} all-gather(f32[4,8,8]{2,1,0:T(8,128)S(1)} %get-tuple-element.104), channel_id=2, replica_groups=mesh['group'=4,'tensor'=64] {'tensor'}, dimensions={0}, use_global_device_ids=true | all-gather | bytes 66560 | tf_op jit(solution)/shard_map/all_gather | solution.py:13
  1422.4 117.8 %all-gather.1 = f32[256,8,8]{2,1,0:T(8,128)S(1)} all-gather(f32[4,8,8]{2,1,0:T(8,128)S(1)} %convert_reduce_fusion), channel_id=3, replica_groups=mesh['group'=4,'tensor'=64] {'tensor'}, dimensions={0}, use_global_device_ids=true | all-gather | bytes 66560 | tf_op jit(solution)/shard_map/all_gather | solution.py:13
  1540.5 8.2 slice.101
  1548.7 70.6 %while.14 = (s32[]{:T(128)}, f32[4,8,8]{2,1,0:T(8,128)S(1)}, f32[4,8,8]{2,1,0:T(8,128)S(1)}, f32[4,8,8,128]{3,2,1,0:T(8,128)S(1)}, f32[63,4,8,8]{3,2,1,0:T(8,128...) while((s32[]{:T(128)}, f32[4,8,8]{2,1,0:T(8,128)S(1)}, ...), condition=%wide.region_8.0_spmd, body=%wide.region_7.0_spmd.sunk | while | flops 99842 | bytes 403557 | solution.py:16
  1548.7 1.1 fusion.46
  1549.8 1.1 fusion.46
  1619.8 1.6 fusion.32
  1621.4 390.0 %psum.63 = bf16[4,5120]{1,0:T(4,128)(2,1)} all-reduce(f32[4,5120]{1,0:T(4,128)S(1)} %fusion.32), channel_id=1, replica_groups=mesh['group'=4,'tensor'=64] {'tensor'}, use_global_device_ids=true, to_apply=%region_23.24 | all-reduce | flops 20480 | bytes 122880 | tf_op jit(solution)/shard_map/psum | solution.py:158
  (208 shorter events, 75.5 us)
Async XLA Ops:
  6.5 857.2 %copy-start = (bf16[4,8,64,128]{3,2,1,0:T(8,128)(2,1)S(1)}, bf16[4,8,64,128]{3,2,1,0:T(8,128)(2,1)}, u32[]{:S(2)}) copy-start(bf16[4,8,64,128]{3,2,1,0:T(8,128)(2,1)} %param.33) | copy-start | bytes 1572868
  6.5 99.8 %copy-start.1 = (bf16[20,8192]{1,0:T(8,128)(2,1)S(1)}, bf16[20,8192]{1,0:T(8,128)(2,1)}, u32[]{:S(2)}) copy-start(bf16[20,8192]{1,0:T(8,128)(2,1)} %param.21) | copy-start | bytes 983044
  6.5 99.8 %copy-start.2 = (bf16[20,8192]{1,0:T(8,128)(2,1)S(1)}, bf16[20,8192]{1,0:T(8,128)(2,1)}, u32[]{:S(2)}) copy-start(bf16[20,8192]{1,0:T(8,128)(2,1)} %param.20) | copy-start | bytes 983044
  6.5 99.8 %copy-start.3 = (bf16[20,8192]{1,0:T(8,128)(2,1)S(1)}, bf16[20,8192]{1,0:T(8,128)(2,1)}, u32[]{:S(2)}) copy-start(bf16[20,8192]{1,0:T(8,128)(2,1)} %param.19) | copy-start | bytes 983044
  6.5 11.5 copy-start.4
  6.5 137.6 %all-gather.14.cloned.1.call-start = ((), (), s32[]{:S(2)}) async-start(), calls=%async_computation.3 | async-start | bytes 1966080 | tf_op jit(solution)/shard_map/all_gather | solution.py:116
  18.0 89.4 %copy-start.15 = (s32[4]{0:T(128)S(1)}, s32[4]{0:T(128)}, u32[]{:S(2)}) copy-start(s32[4]{0:T(128)} %param.34) | copy-start | bytes 52
  18.0 89.4 %copy-start.14 = (bf16[4,5120]{1,0:T(4,128)(2,1)S(1)}, bf16[4,5120]{1,0:T(4,128)(2,1)}, u32[]{:S(2)}) copy-start(bf16[4,5120]{1,0:T(4,128)(2,1)} %param.31) | copy-start | bytes 122884
  107.3 754.8 %all-reduce.4.cloned.1.call-start = ((), (), s32[]{:S(2)}) async-start(), calls=%async_computation | async-start | bytes 262144 | tf_op jit(solution)/shard_map/psum | solution.py:124
  145.7 1.1 copy-start.16
  145.7 717.5 %copy-start.7 = (bf16[4,8,64,128]{3,2,1,0:T(8,128)(2,1)S(1)}, bf16[4,8,64,128]{3,2,1,0:T(8,128)(2,1)}, u32[]{:S(2)}) copy-start(bf16[4,8,64,128]{3,2,1,0:T(8,128)(2,1)} %param.32) | copy-start | bytes 1572868
  146.0 721.7 %copy-start.5 = (bf16[32,5120]{1,0:T(8,128)(2,1)S(1)}, bf16[32,5120]{1,0:T(8,128)(2,1)}, u32[]{:S(2)}) copy-start(bf16[32,5120]{1,0:T(8,128)(2,1)} %param.29) | copy-start | bytes 983044
  146.0 721.7 %copy-start.6 = (bf16[32,5120]{1,0:T(8,128)(2,1)S(1)}, bf16[32,5120]{1,0:T(8,128)(2,1)}, u32[]{:S(2)}) copy-start(bf16[32,5120]{1,0:T(8,128)(2,1)} %param.30) | copy-start | bytes 983044
  146.7 1393.7 %all-gather.12.cloned.1.call-start = ((), (), s32[]{:S(2)}) async-start(), calls=%async_computation.2 | async-start | bytes 8519680 | tf_op jit(solution)/shard_map/all_gather | solution.py:13
  863.8 9.5 copy-start.8
  863.8 9.5 copy-start.9
  863.8 9.5 copy-start.10
  863.8 9.5 copy-start.11
  863.8 9.5 copy-start.12
  863.8 9.5 copy-start.13
  864.8 755.0 %all-gather.10.cloned.1.call-start = ((), (), s32[]{:S(2)}) async-start(), calls=%async_computation.1 | async-start | bytes 1638400 | tf_op jit(solution)/shard_map/all_gather | solution.py:119
  1540.5 8.2 slice-start
Sparse Core Ops, SparseCore 0:
  107.5 36.6 all-gather.13
  146.8 715.2 all-reduce.3
  866.2 113.9 all-gather.11
  982.0 31.3 all-gather.9
where the time goes:
time: 2030 us; the launch traced here: 2020 us
  blocking collectives  1140 us (56%)
  waiting for transfers between devices  751 us (37%)
  other arithmetic  88.3 us (4%)
  between operations  22.4 us (1%)
    psum x1, waiting for transfers between devices, shards(): lax.psum((query_part, key_part, value_part), 'tensor')  715 us
    psum x1, blocking collectives, shards(): lax.psum((query_part, key_part, value_part), 'tensor')  403 us
    psum x1, blocking collectives, shards(): return lax.psum(out_part, 'tensor').astype(jnp.bfloat16)  390 us
    all_gather x2, blocking collectives, combined_all(): pieces = jax.tree.map(lambda part: lax.all_gather(part, axis), value)  240 us
    psum x1, blocking collectives, shards(): sums = lax.psum(piece[3], ('group', 'tensor'))  81.4 us
    add x63, other arithmetic, merge_parts(): left[2] * left_factor[..., None] + right[2] * right_factor[..., None]  67.6 us
  transfers between devices with their start and end apart: 4, of which 2 were waited for; matrix products, arithmetic and copies ran while one was open for 4% of the time, Pallas kernels for 0%

commit v1 on v0

v1 whole, which is shorter than its diff:
```python
import math

import jax
import jax.numpy as jnp
import numpy as np
from jax import lax
from jax.experimental import pallas as pl
from jax.experimental.pallas import tpu as pltpu
from jax.sharding import PartitionSpec as P

MESH = pl.DeviceIdType.MESH
F32 = jnp.float32
BF16 = jnp.bfloat16
G, XY, W = 4, 16, 4
R, HD, SPAN = 4, 128, 64
QW, KW, OW = 8192, 1024, 5120
DEPTH, ODEPTH = 20, 32
SCALE = 1.0 / math.sqrt(HD)


def kernel(
    qi, qf, qs, ki, kf, ks, vi, vf, vs, oi, of, os_, hid, ck, cv, pos, lens, freq,
    out,
    wq, wk, wv, wo, pq, pk, pv, po, kc, vc, hv,
    hsend, hrecv, hfull, sa, ra, sb, rb, mq, mkv, mo,
    qsend, qrecv, zsend, zrecv, slab, qb, qk,
    asend, arecv, xsend, xrecv, hd, bsend, brecv, ysend, yrecv, osend, obuf,
    load_sem, swap_send, swap_recv, send_sem, recv_sem,
):
    g = lax.axis_index("group")
    t = lax.axis_index("tensor")
    xy, w = t // 4, t % 4
    zh, c = w // 2, w % 2
    x = xy // 4
    z = zh * 4 + g

    def remote(src, dst, stage, device):
        return pltpu.make_async_remote_copy(
            src_ref=src, dst_ref=dst, send_sem=send_sem.at[stage], recv_sem=recv_sem.at[stage],
            device_id=device, device_id_type=MESH,
        )

    def settle(ref, sem):
        pltpu.make_async_copy(ref, ref, sem).wait()

    raw = [(qi, qf, qs), (ki, kf, ks), (vi, vf, vs), (oi, of, os_)]
    mine = [wq, wk, wv, wo]
    theirs = [pq, pk, pv, po]
    loads = []
    for m in range(4):
        for j in range(3):
            loads.append(pltpu.make_async_copy(raw[m][j], mine[m].at[j], load_sem.at[3 * m + j]))
    loads.append(pltpu.make_async_copy(ck, kc, load_sem.at[12]))
    loads.append(pltpu.make_async_copy(cv, vc, load_sem.at[13]))
    loads.append(pltpu.make_async_copy(hid, hv, load_sem.at[14]))
    for copy in loads:
        copy.start()

    def plane(i):
        place = (xy * 2 + c + i) % 32
        return (g, (place // 2) * 4 + zh * 2 + place % 2)

    def column(i):
        place = (g * 4 + w + i) % 16
        return (place // 4, xy * 4 + place % 4)

    barrier = pltpu.get_barrier_semaphore()

    def greet_plane(i, _):
        pl.semaphore_signal(barrier, inc=1, device_id=plane(i), device_id_type=MESH)
        return 0

    def greet_column(i, _):
        place = (g * 4 + w + i) % 16
        there = (place // 4, xy * 4 + place % 4)
        chip = (place // 4 == g) & ((place % 4) // 2 == zh)

        @pl.when(jnp.logical_not(chip))
        def _():
            pl.semaphore_signal(barrier, inc=1, device_id=there, device_id_type=MESH)

        return 0

    lax.fori_loop(1, 32, greet_plane, 0)
    lax.fori_loop(1, 16, greet_column, 0)
    pl.semaphore_wait(barrier, 45)

    other = (g, t + 1 - 2 * c)
    swaps = []
    for m, width in enumerate((QW // 2, KW // 2, KW // 2, OW // 2)):
        for j in range(3):
            start = pl.multiple_of((1 - c) * width, 128)
            swaps.append(
                pltpu.make_async_remote_copy(
                    src_ref=raw[m][j].at[:, pl.ds(start, width)], dst_ref=theirs[m].at[j],
                    send_sem=swap_send.at[3 * m + j], recv_sem=swap_recv.at[3 * m + j],
                    device_id=other, device_id_type=MESH,
                )
            )
    for copy in swaps:
        copy.start()

    loads[14].wait()
    place = 40 * (t // 2)
    base = jnp.minimum(place // 128, 8) * 128
    lane = lax.broadcasted_iota(jnp.int32, (256, 128), 1)
    row = lax.broadcasted_iota(jnp.int32, (256, 128), 0)
    piece, step = lane // 32, lane % 32
    wanted = place - base + step + 20 * jnp.where(piece == 0, c, 1 - c)
    pick = jnp.where((row == wanted) & (lane < 64) & (step < 20), 1.0, 0.0).astype(BF16)
    for to in range(G):
        window = hv[:, pl.ds(pl.multiple_of(1280 * to + base, 128), 256)]
        hsend[to] = jnp.dot(window, pick, preferred_element_type=F32)
    for i in range(1, G):
        to = (g + i) % G
        remote(hsend.at[to], hrecv.at[g], 0, (to, t)).start()
    hrecv[g] = hsend[g]

    def sums(ref, rows, width, step):
        def body(i, acc):
            at = pl.ds(pl.multiple_of(i * step, step), step)
            init = ref[0, :, at].astype(F32)
            a = ref[1, :, at].astype(F32) - init
            b = ref[2, :, at].astype(F32) - init
            return (acc[0] + a * a, acc[1] + b * b, acc[2] + a * b)

        zero = jnp.zeros((rows, step), F32)
        totals = lax.fori_loop(0, width // step, body, (zero, zero, zero), unroll=2)
        done = []
        for total in totals:
            line = jnp.sum(total, axis=0, keepdims=True)
            done.append(sum(line[:, 128 * j : 128 * (j + 1)] for j in range(step // 128)))
        return done

    sub16 = lax.broadcasted_iota(jnp.int32, (16, 128), 0)
    lane16 = lax.broadcasted_iota(jnp.int32, (16, 128), 1)
    stack = jnp.zeros((16, 128), F32)
    for m, (ref, rows, width) in enumerate(
        ((wq, DEPTH, QW), (wk, DEPTH, KW), (wv, DEPTH, KW), (wo, ODEPTH, OW))
    ):
        for j in range(3):
            loads[3 * m + j].wait()
        for kind, line in enumerate(sums(ref, rows, width, 256)):
            stack = jnp.where(sub16 == 4 * kind + m, line, stack)
    stack = jnp.sum(stack, axis=1, keepdims=True)
    sa[...] = jnp.sum(jnp.where(sub16 == lane16, stack, 0.0), axis=0, keepdims=True)

    def to_plane(src, dst, stage):
        def body(i, _):
            there = (xy + i) % XY
            remote(src(there), dst, stage, (g, there * 4 + w)).start()
            return 0

        lax.fori_loop(1, XY, body, 0)

    to_plane(lambda there: sa, ra.at[xy], 1)
    ra[xy] = sa[...]
    settle(ra.at[pl.ds(0, XY - 1)], recv_sem.at[1])
    sb[...] = jnp.sum(ra[...], axis=0)

    def send_sums(i, _):
        remote(sb, rb.at[g * 4 + w], 2, column(i)).start()
        return 0

    lax.fori_loop(1, 16, send_sums, 0)
    rb[g * 4 + w] = sb[...]

    mq[...] = jnp.zeros_like(mq)
    mkv[...] = jnp.zeros_like(mkv)
    settle(hrecv.at[pl.ds(0, G - 1)], recv_sem.at[0])
    for i in range(G):
        hfull[4 * i : 4 * i + 4, :] = hrecv[i]
    rows_all = hfull[...].astype(BF16)[:, :64]
    angle_row = lax.broadcasted_iota(jnp.int32, (R, HD), 0)
    at = jnp.zeros((R, HD), F32)
    length = jnp.zeros((32, 256), jnp.int32)
    row32 = lax.broadcasted_iota(jnp.int32, (32, 256), 0) % R
    for r in range(R):
        at = jnp.where(angle_row == r, pos[r].astype(F32), at)
        length = jnp.where(row32 == r, lens[r], length)
    angle = at * freq[...]
    half = lax.broadcasted_iota(jnp.int32, (R, HD), 1) < HD // 2
    cosine = jnp.cos(angle)
    sine = jnp.sin(angle)
    sine = jnp.where(half, -sine, sine)

    def rotate(value):
        return value * cosine + pltpu.roll(value, HD // 2, 1) * sine

    for copy in swaps:
        copy.wait_recv()
    settle(rb.at[pl.ds(0, 15)], recv_sem.at[2])
    total = jnp.broadcast_to(jnp.sum(rb[...], axis=0), (8, 128))
    bb = pltpu.roll(total, 124, 1)
    ab = pltpu.roll(total, 120, 1)
    similar = ab / jnp.sqrt(total * bb + 1e-06)
    share = 1.0 / jnp.sqrt(2.0 * (1.0 + similar))
    lane8 = lax.broadcasted_iota(jnp.int32, (8, 128), 1)
    shares = [
        jnp.sum(jnp.where(lane8 == m, share, 0.0), axis=1, keepdims=True)[0:1] for m in range(4)
    ]

    def merge(init, first, second, factor):
        base = init.astype(F32)
        a = first.astype(F32) - base
        b = second.astype(F32) - base
        return (base + factor * a + factor * b).astype(BF16)

    def merge_into(dst, rows, offset, own, swapped, own_row, other_row, width, factor, step):
        def body(i, _):
            there = pl.ds(pl.multiple_of(i * step, step), step)
            here = pl.ds(pl.multiple_of(c * width + i * step, step), step)
            to = pl.ds(pl.multiple_of(offset + i * step, step), step)
            dst[own_row, to] = merge(own[0, :, here], own[1, :, here], own[2, :, here], factor)
            dst[other_row, to] = merge(
                swapped[0, :, there], swapped[1, :, there], swapped[2, :, there], factor
            )
            return 0

        lax.fori_loop(0, width // step, body, 0, unroll=2)

    top, bottom = pl.ds(0, DEPTH), pl.ds(32, DEPTH)
    merge_into(mq, DEPTH, 0, wq, pq, top, bottom, QW // 2, shares[0], 256)
    merge_into(mkv, DEPTH, 0, wk, pk, top, bottom, KW // 2, shares[1], 256)
    merge_into(mkv, DEPTH, KW // 2, wv, pv, top, bottom, KW // 2, shares[2], 256)

    new = jnp.dot(rows_all, mkv[...], preferred_element_type=F32)
    for to in range(XY):
        for j in range(2):
            part = jnp.dot(
                rows_all, mq[:, 2048 * j + 128 * to : 2048 * j + 128 * (to + 1)],
                preferred_element_type=F32,
            )
            for i in range(G):
                qsend[to, 4 * j + i] = part[4 * i : 4 * i + 4]
        tile = new[:, 128 * (to // 2) : 128 * (to // 2 + 1)]
        for i in range(2):
            start = 8 * (to % 2) + 4 * i
            qsend[to, 8 + i] = tile[start : start + 4]
    to_plane(lambda there: qsend.at[there], qrecv.at[xy], 3)
    qrecv[xy] = qsend[xy]

    merge_into(
        mo, ODEPTH, 0, wo, po, pl.ds(pl.multiple_of(32 * c, 32), 32),
        pl.ds(pl.multiple_of(32 * (1 - c), 32), 32), OW // 2, shares[3], 256,
    )

    settle(qrecv.at[pl.ds(0, XY - 1)], recv_sem.at[3])
    total = jnp.sum(qrecv[...], axis=0)
    for i in range(G):
        zsend[i, 0] = total[i]
        zsend[i, 1] = total[4 + i]
        zsend[i, 2] = total[8 + i % 2]

    def to_z(src, dst, stage):
        def body(i, _):
            there = (z + i) % 8
            group = there % 4
            remote(src(group), dst, stage, (group, xy * 4 + (there // 4) * 2 + c)).start()
            return 0

        lax.fori_loop(1, 8, body, 0)

    to_z(lambda group: zsend.at[group], zrecv.at[z], 4)
    zrecv[z] = zsend[g]
    settle(zrecv.at[pl.ds(0, 7)], recv_sem.at[4])
    total = jnp.sum(zrecv[...], axis=0)
    rounded = lambda value: value.astype(BF16).astype(F32)
    slab[0] = rounded(rotate(total[0]))
    slab[1] = rounded(rotate(total[1]))
    slab[2] = rounded(jnp.where(xy < 8, rotate(total[2]), total[2]))

    def to_everyone(src, dst, stage):
        def body(i, _):
            remote(src, dst, stage, plane(i)).start()
            return 0

        lax.fori_loop(1, 32, body, 0)

    to_everyone(slab, qb.at[c * 16 + xy], 5)
    qb[c * 16 + xy] = slab[...]
    loads[12].wait()
    loads[13].wait()
    settle(qb.at[pl.ds(0, 31)], recv_sem.at[5])

    lane = lax.broadcasted_iota(jnp.int32, (32, 256), 1)
    valid = (lane // SPAN == row32) & (t * SPAN + lane % SPAN < length)
    lane32 = lax.broadcasted_iota(jnp.int32, (32, 128), 1)
    for high in range(2):
        stats = jnp.zeros((32, 128), F32)
        for gamma in range(4):
            half_c, j = gamma // 2, gamma % 2
            k = 2 * gamma + high
            for i in range(8):
                qk[k, 4 * i : 4 * i + 4, :] = qb[half_c * 16 + 8 * high + i, j]
            keys = kc[:, k].reshape(R * SPAN, HD)
            values = vc[:, k].reshape(R * SPAN, HD)
            score = lax.dot_general(
                qk[k].astype(BF16), keys, (((1,), (1,)), ((), ())), preferred_element_type=F32
            )
            score = jnp.where(valid, score * SCALE, -1e30)
            peak = jnp.max(score, axis=1, keepdims=True)
            weight = jnp.where(valid, jnp.exp(score - peak), 0.0).astype(BF16)
            mass = jnp.sum(weight.astype(F32), axis=1, keepdims=True)
            mixed = jnp.dot(weight, values, preferred_element_type=F32)
            for i in range(8):
                asend[8 * high + i, gamma] = mixed[4 * i : 4 * i + 4]
            stats = jnp.where(lane32 == gamma, peak, stats)
            stats = jnp.where(lane32 == 64 + gamma, mass, stats)
        for i in range(8):
            asend[8 * high + i, 4] = stats[4 * i : 4 * i + 4]
    to_plane(lambda there: asend.at[there], arecv.at[xy], 6)
    arecv[xy] = asend[xy]

    k = 2 * w + xy // 8
    query = qb[zh * 16 + xy, c]
    first = (k // 4) * 16 + 2 * (k % 4) + g // 2
    new_key = qb[first, 2]
    new_value = qb[first + 8, 2]
    own = jnp.sum(query * new_key, axis=1, keepdims=True) * SCALE

    settle(arecv.at[pl.ds(0, XY - 1)], recv_sem.at[6])
    stats = arecv[:, 4]
    peaks = jnp.max(stats, axis=0)
    factors = jnp.exp(stats - peaks)
    mass = jnp.zeros((R, HD), F32)
    for i in range(XY):
        mass = mass + factors[i] * pltpu.roll(stats[i], 64, 1)
    lane4 = lax.broadcasted_iota(jnp.int32, (R, HD), 1)
    for gamma in range(4):
        mixed = jnp.zeros((R, HD), F32)
        for i in range(XY):
            mixed = mixed + arecv[i, gamma] * factors[i][:, gamma : gamma + 1]
        peak = peaks[:, gamma : gamma + 1]
        here = w == gamma
        added = jnp.where(here, own, peak)
        most = jnp.maximum(peak, added)
        old = jnp.exp(peak - most)
        fresh = jnp.where(here, jnp.exp(added - most), 0.0)
        xsend[gamma, 0] = mixed * old + fresh * new_value
        xsend[gamma, 1] = jnp.where(lane4 < 64, most, mass[:, gamma : gamma + 1] * old + fresh)

    def send_heads(i, _):
        there = column(i)
        remote(xsend.at[there[0]], xrecv.at[g * 4 + w], 7, there).start()
        return 0

    lax.fori_loop(1, 16, send_heads, 0)
    xrecv[g * 4 + w] = xsend[g]
    settle(xrecv.at[pl.ds(0, 15)], recv_sem.at[7])
    for i in range(G):
        peak = [xrecv[4 * i + j, 1][:, 0:1] for j in range(W)]
        mass = [xrecv[4 * i + j, 1][:, 64:65] for j in range(W)]
        most = jnp.maximum(jnp.maximum(peak[0], peak[1]), jnp.maximum(peak[2], peak[3]))
        factor = [jnp.exp(p - most) for p in peak]
        bottom = sum(f * l for f, l in zip(factor, mass))
        top = sum(f * xrecv[4 * i + j, 0] for j, f in enumerate(factor))
        hd[4 * i : 4 * i + 4, :] = top / bottom
    heads = hd[...]
    heads = jnp.where(zh == 1, pltpu.roll(heads, 64, 1), heads).astype(BF16)[:, :64]

    for tile in range(20):
        part = jnp.dot(
            heads, mo[:, 128 * tile : 128 * (tile + 1)], preferred_element_type=F32
        )
        for i in range(G):
            if tile < XY:
                bsend[tile, i] = part[4 * i : 4 * i + 4]
            else:
                bsend[4 * i + tile - XY, 4] = part[4 * i : 4 * i + 4]
    to_plane(lambda there: bsend.at[there], brecv.at[xy], 8)
    brecv[xy] = bsend[xy]
    settle(brecv.at[pl.ds(0, XY - 1)], recv_sem.at[8])
    total = jnp.sum(brecv[...], axis=0)
    for i in range(G):
        ysend[i, 0] = total[i]
        ysend[i, 1] = total[4]
    to_z(lambda group: ysend.at[group], yrecv.at[z], 9)
    yrecv[z] = ysend[g]
    settle(yrecv.at[pl.ds(0, 7)], recv_sem.at[9])
    osend[...] = jnp.sum(yrecv[...], axis=0)
    to_everyone(osend, obuf.at[c * 16 + xy], 10)
    obuf[c * 16 + xy] = osend[...]
    settle(obuf.at[pl.ds(0, 31)], recv_sem.at[10])
    for half_c in range(2):
        for tile in range(20):
            start = half_c * (OW // 2) + 128 * tile
            if tile < XY:
                value = obuf[half_c * 16 + tile, 0]
            else:
                value = obuf[half_c * 16 + 4 * g + tile - XY, 1]
            out[:, start : start + 128] = value.astype(out.dtype)

    for copy in swaps:
        copy.wait_send()
    for stage, ref, count in (
        (0, hrecv, 3), (1, ra, 15), (2, rb, 15), (3, qrecv, 15), (4, zrecv, 7), (5, qb, 31),
        (6, arecv, 15), (7, xrecv, 15), (8, brecv, 15), (9, yrecv, 7), (10, obuf, 31),
    ):
        settle(ref.at[pl.ds(0, count)], send_sem.at[stage])


def shards(*args):
    freq = 1000000.0 ** (-np.arange(HD // 2) / (HD // 2))
    freq = jnp.asarray(np.concatenate([freq, freq])[None, :], F32)
    any_, vmem, smem = (
        pl.BlockSpec(memory_space=space) for space in (pl.ANY, pltpu.VMEM, pltpu.SMEM)
    )
    f32 = lambda *shape: pltpu.VMEM(shape, F32)
    bf16 = lambda *shape: pltpu.VMEM(shape, BF16)
    return pl.pallas_call(
        kernel,
        out_shape=jax.ShapeDtypeStruct((R, OW), BF16),
        in_specs=[any_] * 15 + [smem] * 2 + [vmem],
        out_specs=vmem,
        scratch_shapes=[
            bf16(3, DEPTH, QW), bf16(3, DEPTH, KW), bf16(3, DEPTH, KW), bf16(3, ODEPTH, OW),
            bf16(3, DEPTH, QW // 2), bf16(3, DEPTH, KW // 2), bf16(3, DEPTH, KW // 2), bf16(3, ODEPTH, OW // 2),
            bf16(R, 8, SPAN, HD), bf16(R, 8, SPAN, HD), bf16(R, 5120),
            f32(G, R, HD), f32(G, R, HD), f32(16, HD),
            f32(1, HD), f32(XY, 1, HD), f32(1, HD), f32(16, 1, HD),
            bf16(64, QW // 2), bf16(64, KW), bf16(64, OW // 2),
            f32(XY, 10, R, HD), f32(XY, 10, R, HD), f32(G, 3, R, HD), f32(8, 3, R, HD),
            f32(3, R, HD), f32(32, 3, R, HD), f32(8, 32, HD),
            f32(XY, 5, R, HD), f32(XY, 5, R, HD), f32(G, 2, R, HD), f32(16, 2, R, HD), f32(16, HD),
            f32(XY, 5, R, HD), f32(XY, 5, R, HD), f32(G, 2, R, HD), f32(8, 2, R, HD),
            f32(2, R, HD), f32(32, 2, R, HD),
            pltpu.SemaphoreType.DMA((15,)), pltpu.SemaphoreType.DMA((12,)), pltpu.SemaphoreType.DMA((12,)),
            pltpu.SemaphoreType.DMA((11,)), pltpu.SemaphoreType.DMA((11,)),
        ],
        compiler_params=pltpu.CompilerParams(
            collective_id=0, has_side_effects=True, vmem_limit_bytes=48 * 1024 * 1024
        ),
        cost_estimate=pl.CostEstimate(flops=40_000_000, bytes_accessed=4_000_000, transcendentals=100_000),
    )(*args, freq)


def solution(mesh):
    both = P(("group", "tensor"), None)
    cache = P("group", None, "tensor", None)
    in_specs = (both,) * 12 + (P("group", None), cache, cache, P("group"), P("group"))
    return jax.shard_map(
        shards, mesh=mesh, in_specs=in_specs, out_specs=P("group", None), check_vma=False
    )
```

time: 2030 us -> 88 us (0.04)
  blocking collectives: 1140 us -> 0 us
  waiting for transfers between devices: 751 us -> 0 us
  other arithmetic: 88.3 us -> 0 us
  Pallas kernels: 0 us -> 71.1 us
  between operations: 22.4 us -> 0.03 us
    psum x3 -> x0, blocking collectives: 874 us -> none  [the longest x1 403 us: shards(): lax.psum((query_part, key_part, value_part), 'tensor')]
    psum x1 -> x0, waiting for transfers between devices: 715 us -> none  [shards(): lax.psum((query_part, key_part, value_part), 'tensor')]
    all_gather x4 -> x0, blocking collectives: 263 us -> none  [the longest x2 240 us: combined_all(): pieces = jax.tree.map(lambda part: lax.all_gather(part, axis), value)]
    pallas_call x0 -> x1, Pallas kernels: none -> 71.1 us  [shards(): pl.pallas_call(kernel, out_shape=jax.ShapeDtypeStruct((R, OW), BF16), in_...]
    add x128 -> x0, other arithmetic: 69 us -> none  [the longest x63 67.6 us: merge_parts(): left[2] * left_factor[..., None] + right[2] * right_factor[..., None]]
    all_gather x3 -> x0, waiting for transfers between devices: 35.9 us -> none  [the longest x1 35.9 us: shards(): lax.all_gather(merged[0], 'group', axis=0, tiled=True)]
  transfers between devices with their start and end apart: 4 -> 0, of which waited for: 2 -> 0; matrix products, arithmetic and copies ran while one was open for 4% -> 0% of each run, Pallas kernels for 0% -> 0%
where the time goes in v1:
time: 88 us; the launch traced here: 87.2 us
  Pallas kernels  71.1 us (81%)
  local copies, waits for them, and re-layouts  16.1 us (18%)
    pallas_call x1, Pallas kernels, shards(): pl.pallas_call(kernel, out_shape=jax.ShapeDtypeStruct((R, OW), BF16), in_...  71.1 us
    unnamed x37, local copies, waits for them, and re-layouts  16.1 us

profile of v1, /device:TPU:1, one launch (start us, length us, event | category | flops | bytes accessed | tf_op | source)
XLA Modules:
  0.0 87.2 jit_solution(1191205654274104560)
XLA Ops:
  0.0 0.0 copy-start
  0.0 1.0 %copy-done = bf16[4,8,64,128]{3,2,1,0:T(8,128)(2,1)S(1)} copy-done((bf16[4,8,64,128]{3,2,1,0:T(8,128)(2,1)S(1)}, bf16[4,8,64,128]{3,2,1,0:T(8,128)(2,1)}, u32[]{:S(2)}) %copy-start) | copy-done | bytes 524312
  1.0 0.0 copy-start.1
  1.0 1.0 %copy-done.1 = bf16[4,8,64,128]{3,2,1,0:T(8,128)(2,1)S(1)} copy-done((bf16[4,8,64,128]{3,2,1,0:T(8,128)(2,1)S(1)}, bf16[4,8,64,128]{3,2,1,0:T(8,128)(2,1)}, u32[]{:S(2)}) %copy-start.1) | copy-done | bytes 524312
  2.1 0.0 copy-start.2
  2.1 1.0 %copy-done.2 = bf16[20,8192]{1,0:T(8,128)(2,1)S(1)} copy-done((bf16[20,8192]{1,0:T(8,128)(2,1)S(1)}, bf16[20,8192]{1,0:T(8,128)(2,1)}, u32[]{:S(2)}) %copy-start.2) | copy-done | bytes 327704
  3.1 0.0 copy-start.3
  3.1 1.0 %copy-done.3 = bf16[20,8192]{1,0:T(8,128)(2,1)S(1)} copy-done((bf16[20,8192]{1,0:T(8,128)(2,1)S(1)}, bf16[20,8192]{1,0:T(8,128)(2,1)}, u32[]{:S(2)}) %copy-start.3) | copy-done | bytes 327704
  4.1 1.0 %copy-done.4 = bf16[20,8192]{1,0:T(8,128)(2,1)S(1)} copy-done((bf16[20,8192]{1,0:T(8,128)(2,1)S(1)}, bf16[20,8192]{1,0:T(8,128)(2,1)}, u32[]{:S(2)}) %copy-start.4) | copy-done | bytes 327704
  5.1 1.0 %copy-done.5 = bf16[32,5120]{1,0:T(8,128)(2,1)S(1)} copy-done((bf16[32,5120]{1,0:T(8,128)(2,1)S(1)}, bf16[32,5120]{1,0:T(8,128)(2,1)}, u32[]{:S(2)}) %copy-start.5) | copy-done | bytes 327704
  6.0 1.0 %copy-done.6 = bf16[32,5120]{1,0:T(8,128)(2,1)S(1)} copy-done((bf16[32,5120]{1,0:T(8,128)(2,1)S(1)}, bf16[32,5120]{1,0:T(8,128)(2,1)}, u32[]{:S(2)}) %copy-start.6) | copy-done | bytes 327704
  7.0 1.0 %copy-done.7 = bf16[32,5120]{1,0:T(8,128)(2,1)S(1)} copy-done((bf16[32,5120]{1,0:T(8,128)(2,1)S(1)}, bf16[32,5120]{1,0:T(8,128)(2,1)}, u32[]{:S(2)}) %copy-start.7) | copy-done | bytes 327704
  8.0 0.8 copy-done.8
  8.8 0.8 copy-done.9
  9.6 0.8 copy-done.10
  10.4 0.8 copy-done.11
  11.2 0.8 copy-done.12
  12.0 0.8 copy-done.13
  12.8 0.8 copy-done.14
  13.6 0.7 copy-done.15
  14.2 0.7 copy-done.16
  14.9 0.7 copy-done.17
  15.5 71.1 %shard_map.172 = bf16[4,5120]{1,0:T(4,128)(2,1)S(1)} custom-call(bf16[20,8192]{1,0:T(8,128)(2,1)S(1)} %copy-done.2, bf16[20,8192]{1,0:T(8,128)(2,1)S(1)} %copy-done.3, bf16[20,8192]{1,0:T(8,128)(2,1)S(1)} %copy-done.4, bf16[20,1024]{1,0:T(8,128)(2,1)S(1)} %copy-done.8, bf16[20,1024]{1,0:T(8,128)(2,1)S(1)} %copy-done.9, bf16[20,1024]{1,0:T(8,128)(2,1)S(1)} %copy-done.10, ...), custom_call_target="tpu_custom_call" | custom-call | flops 40000000 | bytes 4000000 | tf_op jit(solution)/shard_map/pallas_call | solution.py:411
  86.6 0.6 copy.20
  (14 shorter events, 0.0 us)
Async XLA Ops:
  0.0 1.0 %copy-start = (bf16[4,8,64,128]{3,2,1,0:T(8,128)(2,1)S(1)}, bf16[4,8,64,128]{3,2,1,0:T(8,128)(2,1)}, u32[]{:S(2)}) copy-start(bf16[4,8,64,128]{3,2,1,0:T(8,128)(2,1)} %ck.1) | copy-start | bytes 1572868
  1.0 1.0 %copy-start.1 = (bf16[4,8,64,128]{3,2,1,0:T(8,128)(2,1)S(1)}, bf16[4,8,64,128]{3,2,1,0:T(8,128)(2,1)}, u32[]{:S(2)}) copy-start(bf16[4,8,64,128]{3,2,1,0:T(8,128)(2,1)} %cv.1) | copy-start | bytes 1572868
  2.1 1.0 %copy-start.2 = (bf16[20,8192]{1,0:T(8,128)(2,1)S(1)}, bf16[20,8192]{1,0:T(8,128)(2,1)}, u32[]{:S(2)}) copy-start(bf16[20,8192]{1,0:T(8,128)(2,1)} %qi.1) | copy-start | bytes 983044
  3.1 1.0 %copy-start.3 = (bf16[20,8192]{1,0:T(8,128)(2,1)S(1)}, bf16[20,8192]{1,0:T(8,128)(2,1)}, u32[]{:S(2)}) copy-start(bf16[20,8192]{1,0:T(8,128)(2,1)} %qf.1) | copy-start | bytes 983044
  4.1 1.0 %copy-start.4 = (bf16[20,8192]{1,0:T(8,128)(2,1)S(1)}, bf16[20,8192]{1,0:T(8,128)(2,1)}, u32[]{:S(2)}) copy-start(bf16[20,8192]{1,0:T(8,128)(2,1)} %qs.1) | copy-start | bytes 983044
  5.1 1.0 %copy-start.5 = (bf16[32,5120]{1,0:T(8,128)(2,1)S(1)}, bf16[32,5120]{1,0:T(8,128)(2,1)}, u32[]{:S(2)}) copy-start(bf16[32,5120]{1,0:T(8,128)(2,1)} %oi.1) | copy-start | bytes 983044
  6.0 1.0 %copy-start.6 = (bf16[32,5120]{1,0:T(8,128)(2,1)S(1)}, bf16[32,5120]{1,0:T(8,128)(2,1)}, u32[]{:S(2)}) copy-start(bf16[32,5120]{1,0:T(8,128)(2,1)} %of.1) | copy-start | bytes 983044
  7.0 1.0 %copy-start.7 = (bf16[32,5120]{1,0:T(8,128)(2,1)S(1)}, bf16[32,5120]{1,0:T(8,128)(2,1)}, u32[]{:S(2)}) copy-start(bf16[32,5120]{1,0:T(8,128)(2,1)} %os_.1) | copy-start | bytes 983044
  8.0 0.8 copy-start.8
  8.8 0.8 copy-start.9
  9.6 0.8 copy-start.10
  10.4 0.8 copy-start.11
  11.2 0.8 copy-start.12
  12.0 0.8 copy-start.13
  12.8 0.8 copy-start.14
  13.6 0.7 copy-start.15
  14.2 0.7 copy-start.16
  14.9 0.7 copy-start.17

commit v2 on v1

v2 whole, which is shorter than its diff:
```python
import math

import jax
import jax.numpy as jnp
import numpy as np
from jax import lax
from jax.experimental import pallas as pl
from jax.experimental.pallas import tpu as pltpu
from jax.sharding import PartitionSpec as P

MESH = pl.DeviceIdType.MESH
F32 = jnp.float32
BF16 = jnp.bfloat16
G, XY, W = 4, 16, 4
R, HD, SPAN = 4, 128, 64
QW, KW, OW = 8192, 1024, 5120
DEPTH, ODEPTH = 20, 32
FREQ = (1000000.0 ** (-np.arange(HD // 2) / (HD // 2))).astype(np.float32)
SCALE = 1.0 / math.sqrt(HD)


def kernel(
    qi, qf, qs, ki, kf, ks, vi, vf, vs, oi, of, os_, hid, ck, cv, pos_in, lens_in,
    out,
    pos, lens,
    wq, wk, wv, wo, pq, pk, pv, po, keys, values, hv,
    hsend, hrecv, hfull, sa, ra, sb, rb, mq, mkv, mo,
    qsend, qrecv, ksend, krecv, zsend, zrecv, nsend, nrecv,
    asend, arecv, hd, bsend, brecv, ysend, yrecv, osend, obuf,
    load_sem, swap_send, swap_recv, send_sem, recv_sem,
):
    g = lax.axis_index("group")
    t = lax.axis_index("tensor")
    xy, w = t // 4, t % 4
    zh, c = w // 2, w % 2
    x = xy // 4
    z = zh * 4 + g
    my_row = (xy % 8) // 2
    my_kind = 2 * (xy % 2) + xy // 8
    my_kv = 4 * c + my_kind

    def remote(src, dst, stage, device):
        return pltpu.make_async_remote_copy(
            src_ref=src, dst_ref=dst, send_sem=send_sem.at[stage], recv_sem=recv_sem.at[stage],
            device_id=device, device_id_type=MESH,
        )

    def settle(ref, sem):
        pltpu.make_async_copy(ref, ref, sem).wait()

    raw = [(qi, qf, qs), (ki, kf, ks), (vi, vf, vs), (oi, of, os_)]
    mine = [wq, wk, wv, wo]
    theirs = [pq, pk, pv, po]
    loads = []
    for m in range(4):
        for j in range(3):
            loads.append(pltpu.make_async_copy(raw[m][j], mine[m].at[j], load_sem.at[3 * m + j]))
    place = 2 * xy + c
    loads.append(pltpu.make_async_copy(ck.at[my_row, my_kv], keys.at[place], load_sem.at[12]))
    loads.append(pltpu.make_async_copy(cv.at[my_row, my_kv], values.at[place], load_sem.at[13]))
    loads.append(pltpu.make_async_copy(hid, hv, load_sem.at[14]))
    loads.append(pltpu.make_async_copy(pos_in, pos, load_sem.at[15]))
    loads.append(pltpu.make_async_copy(lens_in, lens, load_sem.at[16]))
    for copy in loads:
        copy.start()

    def plane(i):
        place = (xy * 2 + c + i) % 32
        return (g, (place // 2) * 4 + zh * 2 + place % 2)

    def column(i):
        place = (g * 4 + w + i) % 16
        return (place // 4, xy * 4 + place % 4)

    barrier = pltpu.get_barrier_semaphore()

    def greet(i, _):
        pl.semaphore_signal(barrier, inc=1, device_id=plane(i), device_id_type=MESH)
        return 0

    def greet_column(i, _):
        pl.semaphore_signal(barrier, inc=1, device_id=column(i), device_id_type=MESH)
        return 0

    lax.fori_loop(1, 16, greet_column, 0)
    lax.fori_loop(1, 32, greet, 0)

    loads[14].wait()
    place = 40 * (t // 2)
    base = jnp.minimum(place // 128, 8) * 128
    lane = lax.broadcasted_iota(jnp.int32, (256, 128), 1)
    row = lax.broadcasted_iota(jnp.int32, (256, 128), 0)
    piece, step = lane // 32, lane % 32
    wanted = place - base + step + 20 * jnp.where(piece == 0, c, 1 - c)
    pick = jnp.where((row == wanted) & (lane < 64) & (step < 20), 1.0, 0.0).astype(BF16)
    for to in range(G):
        window = hv[:, pl.ds(pl.multiple_of(1280 * to + base, 128), 256)]
        hsend[to] = jnp.dot(window, pick, preferred_element_type=F32)

    def sums(ref, rows, width, step):
        def body(i, acc):
            at = pl.ds(pl.multiple_of(i * step, step), step)
            init = ref[0, :, at].astype(F32)
            a = ref[1, :, at].astype(F32) - init
            b = ref[2, :, at].astype(F32) - init
            return (acc[0] + a * a, acc[1] + b * b, acc[2] + a * b)

        zero = jnp.zeros((rows, step), F32)
        totals = lax.fori_loop(0, width // step, body, (zero, zero, zero), unroll=2)
        done = []
        for total in totals:
            line = jnp.sum(total, axis=0, keepdims=True)
            done.append(sum(line[:, 128 * j : 128 * (j + 1)] for j in range(step // 128)))
        return done

    sub16 = lax.broadcasted_iota(jnp.int32, (16, 128), 0)
    lane16 = lax.broadcasted_iota(jnp.int32, (16, 128), 1)
    stack = jnp.zeros((16, 128), F32)
    for m, (ref, rows, width) in enumerate(
        ((wq, DEPTH, QW), (wk, DEPTH, KW), (wv, DEPTH, KW), (wo, ODEPTH, OW))
    ):
        for j in range(3):
            loads[3 * m + j].wait()
        for kind, line in enumerate(sums(ref, rows, width, 256)):
            stack = jnp.where(sub16 == 4 * kind + m, line, stack)
    stack = jnp.sum(stack, axis=1, keepdims=True)
    sa[...] = jnp.sum(jnp.where(sub16 == lane16, stack, 0.0), axis=0, keepdims=True)

    pl.semaphore_wait(barrier, 46)

    def to_plane(src, dst, stage):
        def body(i, _):
            there = (xy + i) % XY
            remote(src(there), dst, stage, (g, there * 4 + w)).start()
            return 0

        lax.fori_loop(1, XY, body, 0)

    to_plane(lambda there: sa, ra.at[xy], 1)
    ra[xy] = sa[...]

    other = (g, t + 1 - 2 * c)
    swaps = []
    for m, width in enumerate((QW // 2, KW // 2, KW // 2, OW // 2)):
        for j in range(3):
            start = pl.multiple_of((1 - c) * width, 128)
            swaps.append(
                pltpu.make_async_remote_copy(
                    src_ref=raw[m][j].at[:, pl.ds(start, width)], dst_ref=theirs[m].at[j],
                    send_sem=swap_send.at[3 * m + j], recv_sem=swap_recv.at[3 * m + j],
                    device_id=other, device_id_type=MESH,
                )
            )
    for i in range(1, G):
        to = (g + i) % G
        remote(hsend.at[to], hrecv.at[g], 0, (to, t)).start()
    hrecv[g] = hsend[g]
    for copy in swaps:
        copy.start()

    def send_caches(i, _):
        place = (xy * 2 + c + i) % 32
        there, core = place // 2, place % 2
        row, kv = (there % 8) // 2, 4 * core + 2 * (there % 2) + there // 8
        device = (g, there * 4 + zh * 2 + core)
        remote(ck.at[row, kv], keys.at[2 * xy + c], 5, device).start()
        remote(cv.at[row, kv], values.at[2 * xy + c], 6, device).start()
        return 0

    lax.fori_loop(1, 32, send_caches, 0)

    settle(ra.at[pl.ds(0, XY - 1)], recv_sem.at[1])
    sb[...] = jnp.sum(ra[...], axis=0)

    def send_sums(i, _):
        remote(sb, rb.at[g * 4 + w], 2, column(i)).start()
        return 0

    lax.fori_loop(1, 16, send_sums, 0)
    rb[g * 4 + w] = sb[...]

    mq[...] = jnp.zeros_like(mq)
    mkv[...] = jnp.zeros_like(mkv)
    settle(hrecv.at[pl.ds(0, G - 1)], recv_sem.at[0])
    for i in range(G):
        hfull[4 * i : 4 * i + 4, :] = hrecv[i]
    rows_all = hfull[...].astype(BF16)[:, :64]
    loads[15].wait()
    loads[16].wait()
    turn = lax.broadcasted_iota(jnp.int32, (8, HD), 1)
    freq = jnp.ones((8, HD), F32)
    for j, value in enumerate(FREQ):
        freq = jnp.where(turn % (HD // 2) == j, float(value), freq)
    angle = pos[my_row].astype(F32) * freq
    cosine = jnp.cos(angle)
    sine = jnp.sin(angle)
    sine = jnp.where(turn < HD // 2, -sine, sine)

    def rotate(value):
        return value * cosine + pltpu.roll(value, HD // 2, 1) * sine

    for copy in swaps:
        copy.wait_recv()

    settle(rb.at[pl.ds(0, 15)], recv_sem.at[2])
    total = jnp.broadcast_to(jnp.sum(rb[...], axis=0), (8, 128))
    bb = pltpu.roll(total, 124, 1)
    ab = pltpu.roll(total, 120, 1)
    similar = ab / jnp.sqrt(total * bb + 1e-06)
    share = 1.0 / jnp.sqrt(2.0 * (1.0 + similar))
    lane8 = lax.broadcasted_iota(jnp.int32, (8, 128), 1)
    shares = [
        jnp.sum(jnp.where(lane8 == m, share, 0.0), axis=1, keepdims=True)[0:1] for m in range(4)
    ]

    def merge(init, first, second, factor):
        base = init.astype(F32)
        a = first.astype(F32) - base
        b = second.astype(F32) - base
        return (base + factor * a + factor * b).astype(BF16)

    def merge_into(dst, offset, own, swapped, own_row, other_row, width, factor, step):
        def body(i, _):
            there = pl.ds(pl.multiple_of(i * step, step), step)
            here = pl.ds(pl.multiple_of(c * width + i * step, step), step)
            to = pl.ds(pl.multiple_of(offset + i * step, step), step)
            dst[own_row, to] = merge(own[0, :, here], own[1, :, here], own[2, :, here], factor)
            dst[other_row, to] = merge(
                swapped[0, :, there], swapped[1, :, there], swapped[2, :, there], factor
            )
            return 0

        lax.fori_loop(0, width // step, body, 0, unroll=2)

    top, bottom = pl.ds(0, DEPTH), pl.ds(32, DEPTH)
    merge_into(mq, 0, wq, pq, top, bottom, QW // 2, shares[0], 256)

    flat = qsend.reshape(4 * 16 * 8, HD)
    for kind in range(4):
        for half in range(2):
            start = 1024 * kind + 512 * half
            part = jnp.dot(rows_all, mq[:, start : start + 512], preferred_element_type=F32)
            for j in range(4):
                at = pl.ds(128 * kind + 4 * half + j, 16, stride=8)
                flat[at, :] = part[:, 128 * j : 128 * (j + 1)]

    def piece_for(there):
        return (2 * (there % 2) + there // 8, slice(None), (there % 8) // 2)

    to_plane(lambda there: qsend.at[piece_for(there)], qrecv.at[xy], 3)
    qrecv[xy] = qsend[my_kind, :, my_row]

    merge_into(mkv, 0, wk, pk, top, bottom, KW // 2, shares[1], 256)
    merge_into(mkv, KW // 2, wv, pv, top, bottom, KW // 2, shares[2], 256)
    new = jnp.dot(rows_all, mkv[...], preferred_element_type=F32)
    for kind in range(4):
        for i in range(16):
            for j in range(2):
                start = 512 * j + 128 * kind
                ksend[kind, i // 4, i % 4, j : j + 1] = new[i : i + 1, start : start + 128]
    to_plane(lambda there: ksend.at[piece_for(there)], krecv.at[xy], 11)
    krecv[xy] = ksend[my_kind, :, my_row]

    merge_into(
        mo, 0, wo, po, pl.ds(pl.multiple_of(32 * c, 32), 32),
        pl.ds(pl.multiple_of(32 * (1 - c), 32), 32), OW // 2, shares[3], 256,
    )

    def to_z(src, dst, stage):
        def body(i, _):
            there = (z + i) % 8
            group = there % 4
            remote(src(group), dst, stage, (group, xy * 4 + (there // 4) * 2 + c)).start()
            return 0

        lax.fori_loop(1, 8, body, 0)

    settle(qrecv.at[pl.ds(0, XY - 1)], recv_sem.at[3])
    zsend[...] = jnp.sum(qrecv[...], axis=0)
    to_z(lambda group: zsend.at[group], zrecv.at[z], 4)
    zrecv[z] = zsend[g]
    settle(krecv.at[pl.ds(0, XY - 1)], recv_sem.at[11])
    nsend[...] = jnp.sum(krecv[...], axis=0)
    to_z(lambda group: nsend.at[group], nrecv.at[z], 12)
    nrecv[z] = nsend[g]

    loads[12].wait()
    loads[13].wait()
    settle(keys.at[pl.ds(0, 31)], recv_sem.at[5])
    settle(values.at[pl.ds(0, 31)], recv_sem.at[6])
    settle(zrecv.at[pl.ds(0, 7)], recv_sem.at[4])
    query = rotate(jnp.sum(zrecv[...], axis=0)).astype(BF16)
    length = lens[my_row]
    lane = lax.broadcasted_iota(jnp.int32, (8, 128), 1)
    low = lane < SPAN
    scores, peaks = [], []
    for chunk in range(8):
        score = lax.dot_general(
            query, keys[4 * chunk : 4 * chunk + 4].reshape(4 * SPAN, HD),
            (((1,), (1,)), ((), ())), preferred_element_type=F32,
        )
        for i in range(2):
            slot = (4 * (2 * chunk + i) + 2 * zh) * SPAN + lane
            valid = slot < length
            part = jnp.where(valid, score[:, 128 * i : 128 * (i + 1)] * SCALE, -1e30)
            left = jnp.max(jnp.where(low, part, -1e30), axis=1, keepdims=True)
            right = jnp.max(jnp.where(low, -1e30, part), axis=1, keepdims=True)
            scores.append((part, valid))
            peaks.append(jnp.where(low, left, right))
    most = peaks[0]
    for peak in peaks[1:]:
        most = jnp.maximum(most, peak)
    most = jnp.maximum(most, pltpu.roll(most, 64, 1))
    mass = jnp.zeros((8, 128), F32)
    mixed = jnp.zeros((24, HD), F32)
    for chunk in range(8):
        terms = []
        for i in range(2):
            (part, valid), peak = scores[2 * chunk + i], peaks[2 * chunk + i]
            weight = jnp.where(valid, jnp.exp(part - peak), 0.0).astype(BF16).astype(F32)
            weight = weight * jnp.exp(peak - most)
            mass = mass + weight
            first = weight.astype(BF16)
            rest = weight - first.astype(F32)
            second = rest.astype(BF16)
            third = (rest - second.astype(F32)).astype(BF16)
            terms.append(jnp.concatenate([first, second, third], axis=0))
        mixed = mixed + jnp.dot(
            jnp.concatenate(terms, axis=1),
            values[4 * chunk : 4 * chunk + 4].reshape(4 * SPAN, HD),
            preferred_element_type=F32,
        )
    mixed = mixed[0:8] + mixed[8:16] + mixed[16:24]
    mass = jnp.sum(mass, axis=1, keepdims=True)
    most = most[:, 0:1]

    settle(nrecv.at[pl.ds(0, 7)], recv_sem.at[12])
    new = jnp.sum(nrecv[...], axis=0)
    new_key = jnp.broadcast_to(new[0:1], (8, HD))
    new_key = rotate(new_key).astype(BF16).astype(F32)
    new_value = new[1:2].astype(BF16).astype(F32)
    own = jnp.sum(query.astype(F32) * new_key, axis=1, keepdims=True) * SCALE
    own = jnp.where(zh == 0, own, most)
    peak = jnp.maximum(most, own)
    old = jnp.exp(most - peak)
    fresh = jnp.where(zh == 0, jnp.exp(own - peak), 0.0)
    mixed = mixed * old + fresh * new_value
    stats = jnp.where(low, peak, mass * old + fresh)
    for j in range(8):
        asend[j, 0:1] = mixed[j : j + 1]
        asend[j, 1:2] = stats[j : j + 1]

    owner = my_kv // 2
    slot = (4 * g + my_row) * 2 + zh

    def send_heads(i, _):
        place = (xy % 8 * 4 + w + i) % 32
        j = place // 4
        device = (owner, ((xy // 8) * 8 + j) * 4 + place % 4)
        remote(asend.at[j], arecv.at[slot], 7, device).start()
        return 0

    lax.fori_loop(1, 32, send_heads, 0)

    @pl.when(owner != g)
    def _():
        remote(asend.at[xy % 8], arecv.at[slot], 7, (owner, t)).start()
        settle(arecv, recv_sem.at[7])

    @pl.when(owner == g)
    def _():
        arecv[slot] = asend[xy % 8]
        settle(arecv.at[pl.ds(0, 31)], recv_sem.at[7])

    for i in range(16):
        for side in range(2):
            hd[2 * side, i : i + 1] = arecv[2 * i + side, 0:1]
            hd[2 * side + 1, i : i + 1] = arecv[2 * i + side, 1:2]
    left, right = hd[1], hd[3]
    most = jnp.maximum(left[:, 0:1], right[:, 0:1])
    left_factor = jnp.exp(left[:, 0:1] - most)
    right_factor = jnp.exp(right[:, 0:1] - most)
    heads = (hd[0] * left_factor + hd[2] * right_factor) / (
        left[:, 64:65] * left_factor + right[:, 64:65] * right_factor
    )
    heads = jnp.where(zh == 1, pltpu.roll(heads, 64, 1), heads).astype(BF16)[:, :64]

    for tile in range(20):
        part = jnp.dot(
            heads, mo[:, 128 * tile : 128 * (tile + 1)], preferred_element_type=F32
        )
        for i in range(G):
            if tile < XY:
                bsend[tile, i] = part[4 * i : 4 * i + 4]
            else:
                bsend[4 * i + tile - XY, 4] = part[4 * i : 4 * i + 4]
    to_plane(lambda there: bsend.at[there], brecv.at[xy], 8)
    brecv[xy] = bsend[xy]
    settle(brecv.at[pl.ds(0, XY - 1)], recv_sem.at[8])
    total = jnp.sum(brecv[...], axis=0)
    for i in range(G):
        ysend[i, 0] = total[i]
        ysend[i, 1] = total[4]
    to_z(lambda group: ysend.at[group], yrecv.at[z], 9)
    yrecv[z] = ysend[g]
    settle(yrecv.at[pl.ds(0, 7)], recv_sem.at[9])
    osend[...] = jnp.sum(yrecv[...], axis=0)

    def send_out(i, _):
        remote(osend, obuf.at[c * 16 + xy], 10, plane(i)).start()
        return 0

    lax.fori_loop(1, 32, send_out, 0)
    obuf[c * 16 + xy] = osend[...]
    settle(obuf.at[pl.ds(0, 31)], recv_sem.at[10])
    for core in range(2):
        for tile in range(20):
            start = core * (OW // 2) + 128 * tile
            if tile < XY:
                value = obuf[core * 16 + tile, 0]
            else:
                value = obuf[core * 16 + 4 * g + tile - XY, 1]
            out[:, start : start + 128] = value.astype(out.dtype)

    for copy in swaps:
        copy.wait_send()
    for stage, ref, count in (
        (0, hrecv, 3), (1, ra, 15), (2, rb, 15), (3, qrecv, 15), (4, zrecv, 7), (5, keys, 31),
        (6, values, 31), (8, brecv, 15), (9, yrecv, 7), (10, obuf, 31), (11, krecv, 15), (12, nrecv, 7),
    ):
        settle(ref.at[pl.ds(0, count)], send_sem.at[stage])
    settle(arecv.at[pl.ds(0, 31)], send_sem.at[7])

    @pl.when(owner != g)
    def _():
        settle(arecv.at[0], send_sem.at[7])


def shards(*args):
    hbm, vmem = (pl.BlockSpec(memory_space=space) for space in (pltpu.HBM, pltpu.VMEM))
    f32 = lambda *shape: pltpu.VMEM(shape, F32)
    bf16 = lambda *shape: pltpu.VMEM(shape, BF16)
    return pl.pallas_call(
        kernel,
        out_shape=jax.ShapeDtypeStruct((R, OW), BF16),
        in_specs=[hbm] * 17,
        out_specs=vmem,
        scratch_shapes=[
            pltpu.SMEM((R,), jnp.int32), pltpu.SMEM((R,), jnp.int32),
            bf16(3, DEPTH, QW), bf16(3, DEPTH, KW), bf16(3, DEPTH, KW), bf16(3, ODEPTH, OW),
            bf16(3, DEPTH, QW // 2), bf16(3, DEPTH, KW // 2), bf16(3, DEPTH, KW // 2), bf16(3, ODEPTH, OW // 2),
            bf16(32, SPAN, HD), bf16(32, SPAN, HD), bf16(R, 5120),
            f32(G, R, HD), f32(G, R, HD), f32(16, HD),
            f32(1, HD), f32(XY, 1, HD), f32(1, HD), f32(16, 1, HD),
            bf16(64, QW // 2), bf16(64, KW), bf16(64, OW // 2),
            f32(4, G, R, 8, HD), f32(XY, G, 8, HD), f32(4, G, R, 2, HD), f32(XY, G, 2, HD),
            f32(G, 8, HD), f32(8, 8, HD), f32(G, 2, HD), f32(8, 2, HD),
            f32(8, 2, HD), f32(32, 2, HD), f32(4, 16, HD),
            f32(XY, 5, R, HD), f32(XY, 5, R, HD), f32(G, 2, R, HD), f32(8, 2, R, HD),
            f32(2, R, HD), f32(32, 2, R, HD),
            pltpu.SemaphoreType.DMA((17,)), pltpu.SemaphoreType.DMA((12,)), pltpu.SemaphoreType.DMA((12,)),
            pltpu.SemaphoreType.DMA((13,)), pltpu.SemaphoreType.DMA((13,)),
        ],
        compiler_params=pltpu.CompilerParams(
            collective_id=0, has_side_effects=True, vmem_limit_bytes=56 * 1024 * 1024
        ),
        cost_estimate=pl.CostEstimate(flops=40_000_000, bytes_accessed=4_000_000, transcendentals=100_000),
    )(*args)


def solution(mesh):
    both = P(("group", "tensor"), None)
    cache = P("group", None, "tensor", None)
    in_specs = (both,) * 12 + (P("group", None), cache, cache, P("group"), P("group"))
    return jax.shard_map(
        shards, mesh=mesh, in_specs=in_specs, out_specs=P("group", None), check_vma=False
    )
```

time: 88 us -> 64.7 us (0.74)
  local copies, waits for them, and re-layouts: 16.1 us -> 1.41 us
  Pallas kernels: 71.1 us -> 63.1 us
    unnamed x37 -> x1, local copies, waits for them, and re-layouts: 16.1 us -> 1.41 us
    pallas_call x1, Pallas kernels: 71.1 us -> 63.1 us  [shards(): pl.pallas_call(kernel, out_shape=jax.ShapeDtypeStruct((R, OW), BF16), in_...]
where the time goes in v2:
time: 64.7 us; the launch traced here: 64.5 us
  Pallas kernels  63.1 us (98%)
  local copies, waits for them, and re-layouts  1.41 us (2%)
    pallas_call x1, Pallas kernels, shards(): pl.pallas_call(kernel, out_shape=jax.ShapeDtypeStruct((R, OW), BF16), in_...  63.1 us
    unnamed x1, local copies, waits for them, and re-layouts  1.41 us

profile of v2, /device:TPU:1, one launch (start us, length us, event | category | flops | bytes accessed | tf_op | source)
XLA Modules:
  0.0 64.5 jit_solution(4791754547347288496)
XLA Ops:
  0.0 63.1 %shard_map.163 = bf16[4,5120]{1,0:T(4,128)(2,1)} custom-call(bf16[20,8192]{1,0:T(8,128)(2,1)} %qi.1, bf16[20,8192]{1,0:T(8,128)(2,1)} %qf.1, bf16[20,8192]{1,0:T(8,128)(2,1)} %qs.1, bf16[20,1024]{1,0:T(8,128)(2,1)} %ki.1, bf16[20,1024]{1,0:T(8,128)(2,1)} %kf.1, bf16[20,1024]{1,0:T(8,128)(2,1)} %ks.1, bf16[20,1024]{1,0:T(8,128)(2,1)} %vi.1, ...), custom_call_target="tpu_custom_call" | custom-call | flops 40000000 | bytes 4000000 | tf_op jit(solution)/shard_map/pallas_call | solution.py:443
  63.1 1.4 %copy.19 = bf16[4,5120]{1,0:T(4,128)(2,1)} copy(bf16[4,5120]{1,0:T(4,128)(2,1)} %shard_map.163) | data formatting | bytes 81920

commit v3 on v2

--- a/solution.py
+++ b/solution.py
@@ -16,6 +16,23 @@
 QW, KW, OW = 8192, 1024, 5120
 DEPTH, ODEPTH = 20, 32
 FREQ = (1000000.0 ** (-np.arange(HD // 2) / (HD // 2))).astype(np.float32)
+
+
+def ring(step, size):
+    return min(step, size - step)
+
+
+PLANE = sorted(((a, b) for a in range(4) for b in range(4)), key=lambda s: -ring(s[0], 4) - ring(s[1], 4))
+PLANE_CORES = sorted(
+    ((a, b, k) for a, b in PLANE for k in range(2)),
+    key=lambda s: -ring(s[0], 4) - ring(s[1], 4) - 0.1 * s[2],
+)
+LINE = sorted(range(8), key=lambda s: -ring(s, 8))
+COLUMN = sorted(((a, k) for a in LINE for k in range(2)), key=lambda s: -ring(s[0], 8) - 0.1 * s[1])
+OWNERS = sorted(
+    ((a, b, e, k) for a in range(2) for b in range(4) for e in range(2) for k in range(2)),
+    key=lambda s: -s[0] - ring(s[1], 4) - 3 * s[2] - 0.1 * s[3],
+)
 SCALE = 1.0 / math.sqrt(HD)
 
 
@@ -31,12 +48,12 @@
 ):
     g = lax.axis_index("group")
     t = lax.axis_index("tensor")
-    xy, w = t // 4, t % 4
-    zh, c = w // 2, w % 2
-    x = xy // 4
+    xy, w = lax.div(t, 4), lax.rem(t, 4)
+    zh, c = lax.div(w, 2), lax.rem(w, 2)
+    x, y = lax.div(xy, 4), lax.rem(xy, 4)
     z = zh * 4 + g
-    my_row = (xy % 8) // 2
-    my_kind = 2 * (xy % 2) + xy // 8
+    my_row = 2 * lax.rem(x, 2) + lax.div(y, 2)
+    my_kind = 2 * lax.rem(y, 2) + lax.div(x, 2)
     my_kv = 4 * c + my_kind
 
     def remote(src, dst, stage, device):
@@ -64,26 +81,21 @@
     for copy in loads:
         copy.start()
 
-    def plane(i):
-        place = (xy * 2 + c + i) % 32
-        return (g, (place // 2) * 4 + zh * 2 + place % 2)
-
-    def column(i):
-        place = (g * 4 + w + i) % 16
-        return (place // 4, xy * 4 + place % 4)
+    rem, div = lax.rem, lax.div
+
+    def chip(a, b):
+        return rem(x + a, 4) * 4 + rem(y + b, 4)
+
+    def column(a, k):
+        there = rem(z + a, 8)
+        return (rem(there, 4), xy * 4 + div(there, 4) * 2 + rem(c + k, 2))
 
     barrier = pltpu.get_barrier_semaphore()
-
-    def greet(i, _):
-        pl.semaphore_signal(barrier, inc=1, device_id=plane(i), device_id_type=MESH)
-        return 0
-
-    def greet_column(i, _):
-        pl.semaphore_signal(barrier, inc=1, device_id=column(i), device_id_type=MESH)
-        return 0
-
-    lax.fori_loop(1, 16, greet_column, 0)
-    lax.fori_loop(1, 32, greet, 0)
+    for a, k in COLUMN[:-1]:
+        pl.semaphore_signal(barrier, inc=1, device_id=column(a, k), device_id_type=MESH)
+    for a, b in PLANE[:-1]:
+        there = (g, chip(a, b) * 4 + w)
+        pl.semaphore_signal(barrier, inc=1, device_id=there, device_id_type=MESH)
 
     loads[14].wait()
     place = 40 * (t // 2)
@@ -126,15 +138,12 @@
     stack = jnp.sum(stack, axis=1, keepdims=True)
     sa[...] = jnp.sum(jnp.where(sub16 == lane16, stack, 0.0), axis=0, keepdims=True)
 
-    pl.semaphore_wait(barrier, 46)
+    pl.semaphore_wait(barrier, 30)
 
     def to_plane(src, dst, stage):
-        def body(i, _):
-            there = (xy + i) % XY
+        for a, b in PLANE[:-1]:
+            there = chip(a, b)
             remote(src(there), dst, stage, (g, there * 4 + w)).start()
-            return 0
-
-        lax.fori_loop(1, XY, body, 0)
 
     to_plane(lambda there: sa, ra.at[xy], 1)
     ra[xy] = sa[...]
@@ -152,33 +161,31 @@
                 )
             )
     for i in range(1, G):
-        to = (g + i) % G
+        to = rem(g + i, G)
         remote(hsend.at[to], hrecv.at[g], 0, (to, t)).start()
     hrecv[g] = hsend[g]
     for copy in swaps:
         copy.start()
 
-    def send_caches(i, _):
-        place = (xy * 2 + c + i) % 32
-        there, core = place // 2, place % 2
-        row, kv = (there % 8) // 2, 4 * core + 2 * (there % 2) + there // 8
-        device = (g, there * 4 + zh * 2 + core)
-        remote(ck.at[row, kv], keys.at[2 * xy + c], 5, device).start()
-        remote(cv.at[row, kv], values.at[2 * xy + c], 6, device).start()
-        return 0
-
-    lax.fori_loop(1, 32, send_caches, 0)
-
+    def send_cache(src, dst, stage, core, first, last):
+        for a, b in PLANE[first:last]:
+            to_x, to_y = rem(x + a, 4), rem(y + b, 4)
+            row = 2 * rem(to_x, 2) + div(to_y, 2)
+            kv = 4 * core + 2 * rem(to_y, 2) + div(to_x, 2)
+            device = (g, (4 * to_x + to_y) * 4 + zh * 2 + core)
+            remote(src.at[row, kv], dst.at[2 * xy + c], stage, device).start()
+
+    send_cache(ck, keys, 5, c, 0, 15)
+    send_cache(cv, values, 6, c, 0, 15)
     settle(ra.at[pl.ds(0, XY - 1)], recv_sem.at[1])
     sb[...] = jnp.sum(ra[...], axis=0)
 
-    def send_sums(i, _):
-        remote(sb, rb.at[g * 4 + w], 2, column(i)).start()
-        return 0
-
-    lax.fori_loop(1, 16, send_sums, 0)
+    for a, k in COLUMN[:-1]:
+        remote(sb, rb.at[g * 4 + w], 2, column(a, k)).start()
     rb[g * 4 + w] = sb[...]
 
+    send_cache(ck, keys, 5, 1 - c, 0, 16)
+    send_cache(cv, values, 6, 1 - c, 0, 8)
     mq[...] = jnp.zeros_like(mq)
     mkv[...] = jnp.zeros_like(mkv)
     settle(hrecv.at[pl.ds(0, G - 1)], recv_sem.at[0])
@@ -245,7 +252,7 @@
                 flat[at, :] = part[:, 128 * j : 128 * (j + 1)]
 
     def piece_for(there):
-        return (2 * (there % 2) + there // 8, slice(None), (there % 8) // 2)
+        return (2 * rem(there, 2) + div(there, 8), slice(None), div(rem(there, 8), 2))
 
     to_plane(lambda there: qsend.at[piece_for(there)], qrecv.at[xy], 3)
     qrecv[xy] = qsend[my_kind, :, my_row]
@@ -253,11 +260,11 @@
     merge_into(mkv, 0, wk, pk, top, bottom, KW // 2, shares[1], 256)
     merge_into(mkv, KW // 2, wv, pv, top, bottom, KW // 2, shares[2], 256)
     new = jnp.dot(rows_all, mkv[...], preferred_element_type=F32)
+    flat_new = ksend.reshape(4 * 16 * 2, HD)
     for kind in range(4):
-        for i in range(16):
-            for j in range(2):
-                start = 512 * j + 128 * kind
-                ksend[kind, i // 4, i % 4, j : j + 1] = new[i : i + 1, start : start + 128]
+        for j in range(2):
+            start = 512 * j + 128 * kind
+            flat_new[pl.ds(32 * kind + j, 16, stride=2), :] = new[:, start : start + 128]
     to_plane(lambda there: ksend.at[piece_for(there)], krecv.at[xy], 11)
     krecv[xy] = ksend[my_kind, :, my_row]
 
@@ -267,18 +274,15 @@
     )
 
     def to_z(src, dst, stage):
-        def body(i, _):
-            there = (z + i) % 8
-            group = there % 4
-            remote(src(group), dst, stage, (group, xy * 4 + (there // 4) * 2 + c)).start()
-            return 0
-
-        lax.fori_loop(1, 8, body, 0)
+        for a in LINE[:-1]:
+            device = column(a, 0)
+            remote(src(device[0]), dst, stage, device).start()
 
     settle(qrecv.at[pl.ds(0, XY - 1)], recv_sem.at[3])
     zsend[...] = jnp.sum(qrecv[...], axis=0)
     to_z(lambda group: zsend.at[group], zrecv.at[z], 4)
     zrecv[z] = zsend[g]
+    send_cache(cv, values, 6, 1 - c, 8, 16)
     settle(krecv.at[pl.ds(0, XY - 1)], recv_sem.at[11])
     nsend[...] = jnp.sum(krecv[...], axis=0)
     to_z(lambda group: nsend.at[group], nrecv.at[z], 12)
@@ -350,26 +354,22 @@
         asend[j, 0:1] = mixed[j : j + 1]
         asend[j, 1:2] = stats[j : j + 1]
 
-    owner = my_kv // 2
+    owner = lax.div(my_kv, 2)
     slot = (4 * g + my_row) * 2 + zh
 
-    def send_heads(i, _):
-        place = (xy % 8 * 4 + w + i) % 32
-        j = place // 4
-        device = (owner, ((xy // 8) * 8 + j) * 4 + place % 4)
+    for a, b, e, k in OWNERS[:-1]:
+        j = 4 * rem(x + a, 2) + rem(y + b, 4)
+        device = (owner, (div(x, 2) * 8 + j) * 4 + 2 * rem(zh + e, 2) + rem(c + k, 2))
         remote(asend.at[j], arecv.at[slot], 7, device).start()
-        return 0
-
-    lax.fori_loop(1, 32, send_heads, 0)
 
     @pl.when(owner != g)
     def _():
-        remote(asend.at[xy % 8], arecv.at[slot], 7, (owner, t)).start()
+        remote(asend.at[rem(xy, 8)], arecv.at[slot], 7, (owner, t)).start()
         settle(arecv, recv_sem.at[7])
 
     @pl.when(owner == g)
     def _():
-        arecv[slot] = asend[xy % 8]
+        arecv[slot] = asend[rem(xy, 8)]
         settle(arecv.at[pl.ds(0, 31)], recv_sem.at[7])
 
     for i in range(16):
@@ -406,11 +406,9 @@
     settle(yrecv.at[pl.ds(0, 7)], recv_sem.at[9])
     osend[...] = jnp.sum(yrecv[...], axis=0)
 
-    def send_out(i, _):
-        remote(osend, obuf.at[c * 16 + xy], 10, plane(i)).start()
-        return 0
-
-    lax.fori_loop(1, 32, send_out, 0)
+    for a, b, k in PLANE_CORES[:-1]:
+        device = (g, chip(a, b) * 4 + zh * 2 + rem(c + k, 2))
+        remote(osend, obuf.at[c * 16 + xy], 10, device).start()
     obuf[c * 16 + xy] = osend[...]
     settle(obuf.at[pl.ds(0, 31)], recv_sem.at[10])
     for core in range(2):
@@ -430,6 +428,7 @@
     ):
         settle(ref.at[pl.ds(0, count)], send_sem.at[stage])
     settle(arecv.at[pl.ds(0, 31)], send_sem.at[7])
+
 
     @pl.when(owner != g)
     def _():

time: 64.7 us -> 57.1 us (0.88)
  Pallas kernels: 63.1 us -> 55.5 us
    pallas_call x1, Pallas kernels: 63.1 us -> 55.5 us  [shards(): pl.pallas_call(kernel, out_shape=jax.ShapeDtypeStruct((R, OW), BF16), in_...]
where the time goes in v3:
time: 57.1 us; the launch traced here: 56.9 us
  Pallas kernels  55.5 us (97%)
  local copies, waits for them, and re-layouts  1.41 us (2%)
    pallas_call x1, Pallas kernels, shards(): pl.pallas_call(kernel, out_shape=jax.ShapeDtypeStruct((R, OW), BF16), in_...  55.5 us
    unnamed x1, local copies, waits for them, and re-layouts  1.41 us

profile of v3, /device:TPU:1, one launch (start us, length us, event | category | flops | bytes accessed | tf_op | source)
XLA Modules:
  0.0 56.9 jit_solution(4435331827337419630)
XLA Ops:
  0.0 55.5 %shard_map.163 = bf16[4,5120]{1,0:T(4,128)(2,1)} custom-call(bf16[20,8192]{1,0:T(8,128)(2,1)} %qi.1, bf16[20,8192]{1,0:T(8,128)(2,1)} %qf.1, bf16[20,8192]{1,0:T(8,128)(2,1)} %qs.1, bf16[20,1024]{1,0:T(8,128)(2,1)} %ki.1, bf16[20,1024]{1,0:T(8,128)(2,1)} %kf.1, bf16[20,1024]{1,0:T(8,128)(2,1)} %ks.1, bf16[20,1024]{1,0:T(8,128)(2,1)} %vi.1, ...), custom_call_target="tpu_custom_call" | custom-call | flops 40000000 | bytes 4000000 | tf_op jit(solution)/shard_map/pallas_call | solution.py:442
  55.5 1.4 %copy.19 = bf16[4,5120]{1,0:T(4,128)(2,1)} copy(bf16[4,5120]{1,0:T(4,128)(2,1)} %shard_map.163) | data formatting | bytes 81920

commit v4 on v3

--- a/solution.py
+++ b/solution.py
@@ -23,6 +23,7 @@
 
 
 PLANE = sorted(((a, b) for a in range(4) for b in range(4)), key=lambda s: -ring(s[0], 4) - ring(s[1], 4))
+NEAR = PLANE[-2::-1] + PLANE[-1:]
 PLANE_CORES = sorted(
     ((a, b, k) for a, b in PLANE for k in range(2)),
     key=lambda s: -ring(s[0], 4) - ring(s[1], 4) - 0.1 * s[2],
@@ -43,7 +44,7 @@
     wq, wk, wv, wo, pq, pk, pv, po, keys, values, hv,
     hsend, hrecv, hfull, sa, ra, sb, rb, mq, mkv, mo,
     qsend, qrecv, ksend, krecv, zsend, zrecv, nsend, nrecv,
-    asend, arecv, hd, bsend, brecv, ysend, yrecv, osend, obuf,
+    asend, arecv, hd, bsend, brecv, ysend, yrecv, osend,
     load_sem, swap_send, swap_recv, send_sem, recv_sem,
 ):
     g = lax.axis_index("group")
@@ -168,7 +169,7 @@
         copy.start()
 
     def send_cache(src, dst, stage, core, first, last):
-        for a, b in PLANE[first:last]:
+        for a, b in NEAR[first:last]:
             to_x, to_y = rem(x + a, 4), rem(y + b, 4)
             row = 2 * rem(to_x, 2) + div(to_y, 2)
             kv = 4 * core + 2 * rem(to_y, 2) + div(to_x, 2)
@@ -404,29 +405,51 @@
     to_z(lambda group: ysend.at[group], yrecv.at[z], 9)
     yrecv[z] = ysend[g]
     settle(yrecv.at[pl.ds(0, 7)], recv_sem.at[9])
-    osend[...] = jnp.sum(yrecv[...], axis=0)
-
-    for a, b, k in PLANE_CORES[:-1]:
-        device = (g, chip(a, b) * 4 + zh * 2 + rem(c + k, 2))
-        remote(osend, obuf.at[c * 16 + xy], 10, device).start()
-    obuf[c * 16 + xy] = osend[...]
-    settle(obuf.at[pl.ds(0, 31)], recv_sem.at[10])
-    for core in range(2):
-        for tile in range(20):
-            start = core * (OW // 2) + 128 * tile
-            if tile < XY:
-                value = obuf[core * 16 + tile, 0]
-            else:
-                value = obuf[core * 16 + 4 * g + tile - XY, 1]
-            out[:, start : start + 128] = value.astype(out.dtype)
+    osend[...] = jnp.sum(yrecv[...], axis=0).astype(BF16)
+    whole = pl.ds(pl.multiple_of(c * (OW // 2) + xy * 128, 128), 128)
+    rest = pl.ds(pl.multiple_of(c * (OW // 2) + 2048 + y * 128, 128), 128)
+
+    def everyone():
+        for a, b, k in PLANE_CORES[:-1]:
+            yield (g, chip(a, b) * 4 + zh * 2 + rem(c + k, 2))
+
+    @pl.when(x == g)
+    def _():
+        for device in everyone():
+            remote(osend.at[0], out.at[:, whole], 10, device).start()
+            remote(osend.at[1], out.at[:, rest], 10, device).start()
+        copies = [
+            pltpu.make_async_copy(osend.at[0], out.at[:, whole], load_sem.at[0]),
+            pltpu.make_async_copy(osend.at[1], out.at[:, rest], load_sem.at[1]),
+        ]
+        for copy in copies:
+            copy.start()
+        for copy in copies:
+            copy.wait()
+        settle(out.at[:, pl.ds(0, 38 * 128)], recv_sem.at[10])
+
+    @pl.when(x != g)
+    def _():
+        for device in everyone():
+            remote(osend.at[0], out.at[:, whole], 10, device).start()
+        copy = pltpu.make_async_copy(osend.at[0], out.at[:, whole], load_sem.at[0])
+        copy.start()
+        copy.wait()
+        settle(out.at[:, pl.ds(0, 39 * 128)], recv_sem.at[10])
 
     for copy in swaps:
         copy.wait_send()
     for stage, ref, count in (
         (0, hrecv, 3), (1, ra, 15), (2, rb, 15), (3, qrecv, 15), (4, zrecv, 7), (5, keys, 31),
-        (6, values, 31), (8, brecv, 15), (9, yrecv, 7), (10, obuf, 31), (11, krecv, 15), (12, nrecv, 7),
+        (6, values, 31), (8, brecv, 15), (9, yrecv, 7), (11, krecv, 15), (12, nrecv, 7),
     ):
         settle(ref.at[pl.ds(0, count)], send_sem.at[stage])
+    settle(out.at[:, pl.ds(0, 31 * 128)], send_sem.at[10])
+
+    @pl.when(x == g)
+    def _():
+        settle(out.at[:, pl.ds(0, 31 * 128)], send_sem.at[10])
+
     settle(arecv.at[pl.ds(0, 31)], send_sem.at[7])
 
 
@@ -436,14 +459,14 @@
 
 
 def shards(*args):
-    hbm, vmem = (pl.BlockSpec(memory_space=space) for space in (pltpu.HBM, pltpu.VMEM))
+    hbm = pl.BlockSpec(memory_space=pltpu.HBM)
     f32 = lambda *shape: pltpu.VMEM(shape, F32)
     bf16 = lambda *shape: pltpu.VMEM(shape, BF16)
     return pl.pallas_call(
         kernel,
         out_shape=jax.ShapeDtypeStruct((R, OW), BF16),
         in_specs=[hbm] * 17,
-        out_specs=vmem,
+        out_specs=hbm,
         scratch_shapes=[
             pltpu.SMEM((R,), jnp.int32), pltpu.SMEM((R,), jnp.int32),
             bf16(3, DEPTH, QW), bf16(3, DEPTH, KW), bf16(3, DEPTH, KW), bf16(3, ODEPTH, OW),
@@ -456,7 +479,7 @@
             f32(G, 8, HD), f32(8, 8, HD), f32(G, 2, HD), f32(8, 2, HD),
             f32(8, 2, HD), f32(32, 2, HD), f32(4, 16, HD),
             f32(XY, 5, R, HD), f32(XY, 5, R, HD), f32(G, 2, R, HD), f32(8, 2, R, HD),
-            f32(2, R, HD), f32(32, 2, R, HD),
+            bf16(2, R, HD),
             pltpu.SemaphoreType.DMA((17,)), pltpu.SemaphoreType.DMA((12,)), pltpu.SemaphoreType.DMA((12,)),
             pltpu.SemaphoreType.DMA((13,)), pltpu.SemaphoreType.DMA((13,)),
         ],

time: 57.1 us -> 55.2 us (0.967)
  Pallas kernels: 55.5 us -> 53.6 us
    pallas_call x1, Pallas kernels: 55.5 us -> 53.6 us  [shards(): pl.pallas_call(kernel, out_shape=jax.ShapeDtypeStruct((R, OW), BF16), in_...]
where the time goes in v4:
time: 55.2 us; the launch traced here: 55.1 us
  Pallas kernels  53.6 us (97%)
  local copies, waits for them, and re-layouts  1.41 us (3%)
    pallas_call x1, Pallas kernels, shards(): pl.pallas_call(kernel, out_shape=jax.ShapeDtypeStruct((R, OW), BF16), in_...  53.6 us
    unnamed x1, local copies, waits for them, and re-layouts  1.41 us

profile of v4, /device:TPU:1, one launch (start us, length us, event | category | flops | bytes accessed | tf_op | source)
XLA Modules:
  0.0 55.1 jit_solution(14482504136489807462)
XLA Ops:
  0.0 53.6 %shard_map.163 = bf16[4,5120]{1,0:T(4,128)(2,1)} custom-call(bf16[20,8192]{1,0:T(8,128)(2,1)} %qi.1, bf16[20,8192]{1,0:T(8,128)(2,1)} %qf.1, bf16[20,8192]{1,0:T(8,128)(2,1)} %qs.1, bf16[20,1024]{1,0:T(8,128)(2,1)} %ki.1, bf16[20,1024]{1,0:T(8,128)(2,1)} %kf.1, bf16[20,1024]{1,0:T(8,128)(2,1)} %ks.1, bf16[20,1024]{1,0:T(8,128)(2,1)} %vi.1, ...), custom_call_target="tpu_custom_call" | custom-call | flops 40000000 | bytes 4000000 | tf_op jit(solution)/shard_map/pallas_call | solution.py:465
  53.7 1.4 %copy.19 = bf16[4,5120]{1,0:T(4,128)(2,1)} copy(bf16[4,5120]{1,0:T(4,128)(2,1)} %shard_map.163) | data formatting | bytes 81920

commit v5 on v4

--- a/solution.py
+++ b/solution.py
@@ -464,9 +464,9 @@
     bf16 = lambda *shape: pltpu.VMEM(shape, BF16)
     return pl.pallas_call(
         kernel,
-        out_shape=jax.ShapeDtypeStruct((R, OW), BF16),
+        out_shape=pltpu.VMEM((R, OW), BF16),
         in_specs=[hbm] * 17,
-        out_specs=hbm,
+        out_specs=pl.BlockSpec(memory_space=pl.ANY),
         scratch_shapes=[
             pltpu.SMEM((R,), jnp.int32), pltpu.SMEM((R,), jnp.int32),
             bf16(3, DEPTH, QW), bf16(3, DEPTH, KW), bf16(3, DEPTH, KW), bf16(3, ODEPTH, OW),
@@ -484,10 +484,10 @@
             pltpu.SemaphoreType.DMA((13,)), pltpu.SemaphoreType.DMA((13,)),
         ],
         compiler_params=pltpu.CompilerParams(
-            collective_id=0, has_side_effects=True, vmem_limit_bytes=56 * 1024 * 1024
+            collective_id=0, has_side_effects=True, vmem_limit_bytes=24 * 1024 * 1024
         ),
         cost_estimate=pl.CostEstimate(flops=40_000_000, bytes_accessed=4_000_000, transcendentals=100_000),
-    )(*args)
+    )(*(pltpu.with_memory_space_constraint(arg, pltpu.HBM) for arg in args))
 
 
 def solution(mesh):

time: 55.2 us -> 54.3 us (0.984)
  local copies, waits for them, and re-layouts: 1.41 us -> 0.62 us
    unnamed x1, local copies, waits for them, and re-layouts: 1.41 us -> 0.62 us
where the time goes in v5:
time: 54.3 us; the launch traced here: 54.2 us
  Pallas kernels  53.5 us (99%)
  local copies, waits for them, and re-layouts  0.62 us (1%)
    pallas_call x1, Pallas kernels, shards(): pl.pallas_call(kernel, out_shape=pltpu.VMEM((R, OW), BF16), in_specs=[hbm...  53.5 us

profile of v5, /device:TPU:1, one launch (start us, length us, event | category | flops | bytes accessed | tf_op | source)
XLA Modules:
  0.0 54.2 jit_solution(11027424280032905475)
XLA Ops:
  0.0 53.5 %shard_map.163 = bf16[4,5120]{1,0:T(4,128)(2,1)S(1)} custom-call(bf16[20,8192]{1,0:T(8,128)(2,1)} %qi.1, bf16[20,8192]{1,0:T(8,128)(2,1)} %qf.1, bf16[20,8192]{1,0:T(8,128)(2,1)} %qs.1, bf16[20,1024]{1,0:T(8,128)(2,1)} %ki.1, bf16[20,1024]{1,0:T(8,128)(2,1)} %kf.1, bf16[20,1024]{1,0:T(8,128)(2,1)} %ks.1, bf16[20,1024]{1,0:T(8,128)(2,1)} %vi.1, ...), custom_call_target="tpu_custom_call" | custom-call | flops 40000000 | bytes 4000000 | tf_op jit(solution)/shard_map/pallas_call | solution.py:465
  53.5 0.6 %copy.19 = bf16[4,5120]{1,0:T(4,128)(2,1)} copy(bf16[4,5120]{1,0:T(4,128)(2,1)S(1)} %shard_map.163) | data formatting | bytes 81920

commit v6 on v5

--- a/solution.py
+++ b/solution.py
@@ -218,7 +218,7 @@
     share = 1.0 / jnp.sqrt(2.0 * (1.0 + similar))
     lane8 = lax.broadcasted_iota(jnp.int32, (8, 128), 1)
     shares = [
-        jnp.sum(jnp.where(lane8 == m, share, 0.0), axis=1, keepdims=True)[0:1] for m in range(4)
+        share[0:1, m : m + 1] for m in range(4)
     ]
 
     def merge(init, first, second, factor):
@@ -238,19 +238,18 @@
             )
             return 0
 
-        lax.fori_loop(0, width // step, body, 0, unroll=2)
+        lax.fori_loop(0, width // step, body, 0, unroll=8 if width > 2560 else 2)
 
     top, bottom = pl.ds(0, DEPTH), pl.ds(32, DEPTH)
     merge_into(mq, 0, wq, pq, top, bottom, QW // 2, shares[0], 256)
 
     flat = qsend.reshape(4 * 16 * 8, HD)
     for kind in range(4):
-        for half in range(2):
-            start = 1024 * kind + 512 * half
-            part = jnp.dot(rows_all, mq[:, start : start + 512], preferred_element_type=F32)
-            for j in range(4):
-                at = pl.ds(128 * kind + 4 * half + j, 16, stride=8)
-                flat[at, :] = part[:, 128 * j : 128 * (j + 1)]
+        part = jnp.dot(
+            rows_all, mq[:, 1024 * kind : 1024 * (kind + 1)], preferred_element_type=F32
+        )
+        for j in range(8):
+            flat[pl.ds(128 * kind + j, 16, stride=8), :] = part[:, 128 * j : 128 * (j + 1)]
 
     def piece_for(there):
         return (2 * rem(there, 2) + div(there, 8), slice(None), div(rem(there, 8), 2))
@@ -391,10 +390,12 @@
             heads, mo[:, 128 * tile : 128 * (tile + 1)], preferred_element_type=F32
         )
         for i in range(G):
-            if tile < XY:
-                bsend[tile, i] = part[4 * i : 4 * i + 4]
+            others = [4 * a + b for a in range(4) if a != i for b in range(4)]
+            if tile >= 8:
+                to, at = others[tile - 8], i
             else:
-                bsend[4 * i + tile - XY, 4] = part[4 * i : 4 * i + 4]
+                to, at = 4 * i + tile // 2, (i, 4)[tile % 2]
+            bsend[to, at] = part[4 * i : 4 * i + 4]
     to_plane(lambda there: bsend.at[there], brecv.at[xy], 8)
     brecv[xy] = bsend[xy]
     settle(brecv.at[pl.ds(0, XY - 1)], recv_sem.at[8])
@@ -405,37 +406,32 @@
     to_z(lambda group: ysend.at[group], yrecv.at[z], 9)
     yrecv[z] = ysend[g]
     settle(yrecv.at[pl.ds(0, 7)], recv_sem.at[9])
-    osend[...] = jnp.sum(yrecv[...], axis=0).astype(BF16)
-    whole = pl.ds(pl.multiple_of(c * (OW // 2) + xy * 128, 128), 128)
-    rest = pl.ds(pl.multiple_of(c * (OW // 2) + 2048 + y * 128, 128), 128)
-
-    def everyone():
+    done = jnp.sum(yrecv[...], axis=0).astype(BF16)
+    osend[:, 0:128] = done[0]
+    osend[:, 128:256] = done[1]
+
+    def finish(start, tiles):
+        src = osend.at[:, pl.ds(0, 128 * tiles)]
+        dst = out.at[:, pl.ds(pl.multiple_of(c * (OW // 2) + start, 128), 128 * tiles)]
         for a, b, k in PLANE_CORES[:-1]:
-            yield (g, chip(a, b) * 4 + zh * 2 + rem(c + k, 2))
-
-    @pl.when(x == g)
-    def _():
-        for device in everyone():
-            remote(osend.at[0], out.at[:, whole], 10, device).start()
-            remote(osend.at[1], out.at[:, rest], 10, device).start()
-        copies = [
-            pltpu.make_async_copy(osend.at[0], out.at[:, whole], load_sem.at[0]),
-            pltpu.make_async_copy(osend.at[1], out.at[:, rest], load_sem.at[1]),
-        ]
-        for copy in copies:
-            copy.start()
-        for copy in copies:
-            copy.wait()
-        settle(out.at[:, pl.ds(0, 38 * 128)], recv_sem.at[10])
-
-    @pl.when(x != g)
-    def _():
-        for device in everyone():
-            remote(osend.at[0], out.at[:, whole], 10, device).start()
-        copy = pltpu.make_async_copy(osend.at[0], out.at[:, whole], load_sem.at[0])
+            device = (g, chip(a, b) * 4 + zh * 2 + rem(c + k, 2))
+            remote(src, dst, 10, device).start()
+        copy = pltpu.make_async_copy(src, dst, load_sem.at[0])
         copy.start()
         copy.wait()
-        settle(out.at[:, pl.ds(0, 39 * 128)], recv_sem.at[10])
+        settle(out.at[:, pl.ds(0, (40 - tiles) * 128)], recv_sem.at[10])
+
+    @pl.when(x == g)
+    def _():
+        finish(256 * y, 2)
+
+    @pl.when(x < g)
+    def _():
+        finish(1024 + 128 * xy, 1)
+
+    @pl.when(x > g)
+    def _():
+        finish(512 + 128 * xy, 1)
 
     for copy in swaps:
         copy.wait_send()
@@ -479,7 +475,7 @@
             f32(G, 8, HD), f32(8, 8, HD), f32(G, 2, HD), f32(8, 2, HD),
             f32(8, 2, HD), f32(32, 2, HD), f32(4, 16, HD),
             f32(XY, 5, R, HD), f32(XY, 5, R, HD), f32(G, 2, R, HD), f32(8, 2, R, HD),
-            bf16(2, R, HD),
+            bf16(R, 2 * HD),
             pltpu.SemaphoreType.DMA((17,)), pltpu.SemaphoreType.DMA((12,)), pltpu.SemaphoreType.DMA((12,)),
             pltpu.SemaphoreType.DMA((13,)), pltpu.SemaphoreType.DMA((13,)),
         ],

time: 54.3 us -> 54.2 us (level)
  no operation moved by 1% of the time
where the time goes in v6:
time: 54.2 us; the launch traced here: 54.1 us
  Pallas kernels  53.5 us (99%)
  local copies, waits for them, and re-layouts  0.62 us (1%)
    pallas_call x1, Pallas kernels, shards(): pl.pallas_call(kernel, out_shape=pltpu.VMEM((R, OW), BF16), in_specs=[hbm...  53.5 us

profile of v6, /device:TPU:1, one launch (start us, length us, event | category | flops | bytes accessed | tf_op | source)
XLA Modules:
  0.0 54.1 jit_solution(5353732142279367082)
XLA Ops:
  0.0 53.5 %shard_map.163 = bf16[4,5120]{1,0:T(4,128)(2,1)S(1)} custom-call(bf16[20,8192]{1,0:T(8,128)(2,1)} %qi.1, bf16[20,8192]{1,0:T(8,128)(2,1)} %qf.1, bf16[20,8192]{1,0:T(8,128)(2,1)} %qs.1, bf16[20,1024]{1,0:T(8,128)(2,1)} %ki.1, bf16[20,1024]{1,0:T(8,128)(2,1)} %kf.1, bf16[20,1024]{1,0:T(8,128)(2,1)} %ks.1, bf16[20,1024]{1,0:T(8,128)(2,1)} %vi.1, ...), custom_call_target="tpu_custom_call" | custom-call | flops 40000000 | bytes 4000000 | tf_op jit(solution)/shard_map/pallas_call | solution.py:461
  53.5 0.6 %copy.19 = bf16[4,5120]{1,0:T(4,128)(2,1)} copy(bf16[4,5120]{1,0:T(4,128)(2,1)S(1)} %shard_map.163) | data formatting | bytes 81920

commit v7 on v6

--- a/solution.py
+++ b/solution.py
@@ -403,12 +403,29 @@
     for i in range(G):
         ysend[i, 0] = total[i]
         ysend[i, 1] = total[4]
-    to_z(lambda group: ysend.at[group], yrecv.at[z], 9)
+    for a in LINE[:-1]:
+        device = column(a, 0)
+        group = device[0]
+
+        @pl.when(group == x)
+        def _():
+            remote(ysend.at[group], yrecv.at[z], 9, device).start()
+
+        @pl.when(group != x)
+        def _():
+            remote(ysend.at[group, 0], yrecv.at[z, 0], 9, device).start()
+
     yrecv[z] = ysend[g]
-    settle(yrecv.at[pl.ds(0, 7)], recv_sem.at[9])
-    done = jnp.sum(yrecv[...], axis=0).astype(BF16)
-    osend[:, 0:128] = done[0]
-    osend[:, 128:256] = done[1]
+
+    @pl.when(x == g)
+    def _():
+        settle(yrecv.at[pl.ds(0, 7)], recv_sem.at[9])
+
+    @pl.when(x != g)
+    def _():
+        settle(yrecv.at[pl.ds(0, 7), 0], recv_sem.at[9])
+
+    osend[:, 0:128] = jnp.sum(yrecv[:, 0], axis=0).astype(BF16)
 
     def finish(start, tiles):
         src = osend.at[:, pl.ds(0, 128 * tiles)]
@@ -423,6 +440,7 @@
 
     @pl.when(x == g)
     def _():
+        osend[:, 128:256] = jnp.sum(yrecv[:, 1], axis=0).astype(BF16)
         finish(256 * y, 2)
 
     @pl.when(x < g)
@@ -437,7 +455,7 @@
         copy.wait_send()
     for stage, ref, count in (
         (0, hrecv, 3), (1, ra, 15), (2, rb, 15), (3, qrecv, 15), (4, zrecv, 7), (5, keys, 31),
-        (6, values, 31), (8, brecv, 15), (9, yrecv, 7), (11, krecv, 15), (12, nrecv, 7),
+        (6, values, 31), (8, brecv, 15), (11, krecv, 15), (12, nrecv, 7),
     ):
         settle(ref.at[pl.ds(0, count)], send_sem.at[stage])
     settle(out.at[:, pl.ds(0, 31 * 128)], send_sem.at[10])
@@ -445,6 +463,13 @@
     @pl.when(x == g)
     def _():
         settle(out.at[:, pl.ds(0, 31 * 128)], send_sem.at[10])
+
+    settle(yrecv.at[pl.ds(0, 7), 0], send_sem.at[9])
+    settle(yrecv.at[0, 0], send_sem.at[9])
+
+    @pl.when(x != g)
+    def _():
+        settle(yrecv.at[0, 0], send_sem.at[9])
 
     settle(arecv.at[pl.ds(0, 31)], send_sem.at[7])
 

time: 54.2 us -> 54.2 us (level)
  no operation moved by 1% of the time
where the time goes in v7:
time: 54.2 us; the launch traced here: 54.1 us
  Pallas kernels  53.5 us (99%)
  local copies, waits for them, and re-layouts  0.62 us (1%)
    pallas_call x1, Pallas kernels, shards(): pl.pallas_call(kernel, out_shape=pltpu.VMEM((R, OW), BF16), in_specs=[hbm...  53.5 us

profile of v7, /device:TPU:1, one launch (start us, length us, event | category | flops | bytes accessed | tf_op | source)
XLA Modules:
  0.0 54.1 jit_solution(2521005012155728275)
XLA Ops:
  0.0 53.5 %shard_map.163 = bf16[4,5120]{1,0:T(4,128)(2,1)S(1)} custom-call(bf16[20,8192]{1,0:T(8,128)(2,1)} %qi.1, bf16[20,8192]{1,0:T(8,128)(2,1)} %qf.1, bf16[20,8192]{1,0:T(8,128)(2,1)} %qs.1, bf16[20,1024]{1,0:T(8,128)(2,1)} %ki.1, bf16[20,1024]{1,0:T(8,128)(2,1)} %kf.1, bf16[20,1024]{1,0:T(8,128)(2,1)} %ks.1, bf16[20,1024]{1,0:T(8,128)(2,1)} %vi.1, ...), custom_call_target="tpu_custom_call" | custom-call | flops 40000000 | bytes 4000000 | tf_op jit(solution)/shard_map/pallas_call | solution.py:486
  53.5 0.6 %copy.19 = bf16[4,5120]{1,0:T(4,128)(2,1)} copy(bf16[4,5120]{1,0:T(4,128)(2,1)S(1)} %shard_map.163) | data formatting | bytes 81920
